TPU v7x, 32 devices: a whole 2x2x4 slice. The times are simulated.
32 devices in a mesh: utt: 4 (over y, core), seq: 8 (over z, x).
Axes of the slice: x: 2, y: 2, z: 4, core: 2. Of those that a mesh axis runs over, the one named last changes fastest.
Arguments:
- inputs: bfloat16 [5632, 1024], P(('utt', 'seq')), may hold values from -6 to 6
- skip_in: bfloat16 [5632, 1024], P(('utt', 'seq')), may hold values from -6 to 6
- lengths: int32 [4, 6], P('utt'), may hold values from 1 to 1320, as said below
- cotangent: bfloat16 [5632, 1024], P(('utt', 'seq')), may hold values from -6 to 6
- w_skip: bfloat16 [2048, 1024], replicated, may hold values from -0.125 to 0.125
- gain_one: float32 [1024], replicated, may hold values from 0.25 to 1.75
- w_qkv: bfloat16 [1024, 3072], replicated, may hold values from -0.1875 to 0.1875
- w_out: bfloat16 [1024, 1024], replicated, may hold values from -3 to 3
- gain_two: float32 [1024], replicated, may hold values from 0.25 to 1.75
- w_up: bfloat16 [1024, 4096], replicated, may hold values from -0.1875 to 0.1875
- b_up: float32 [4096], replicated, may hold values from -3 to 3
- w_down: bfloat16 [4096, 1024], replicated, may hold values from -0.09375 to 0.09375
- b_down: float32 [1024], replicated, may hold values from -3 to 3
Outputs:
- result: bfloat16 [5632, 1024], P(('utt', 'seq'))
- d_inputs: bfloat16 [5632, 1024], P(('utt', 'seq'))
- d_skip: bfloat16 [5632, 1024], P(('utt', 'seq'))
- g_w_skip: float32 [2048, 1024], P('seq')
- g_gain_one: float32 [1024], replicated
- g_w_qkv: float32 [1024, 3072], P('seq')
- g_w_out: float32 [1024, 1024], P('seq')
- g_gain_two: float32 [1024], replicated
- g_w_up: float32 [1024, 4096], P('seq')
- g_b_up: float32 [4096], replicated
- g_w_down: float32 [4096, 1024], P('seq')
- g_b_down: float32 [1024], replicated
Inputs may be any that keep to these rules, and one draw needn't show every extreme that they name: In each group the lengths sum to 1408; exactly one of them, at a slot drawn from the seed, is 1320, and the others sum to 88.
All inputs are finite; a program needn't handle non-finite values.
Results may differ from a plain program's by a relative error of at most 0.02.
Values may be sent and summed in bfloat16 or wider, within the bound.
A program may use at most 192 MiB of HBM per device.

v0:
```python
import functools
import math

import jax
import jax.numpy as jnp
from jax import lax
from jax.experimental import pallas as pl
from jax.experimental.pallas import tpu as pltpu
from jax.sharding import Mesh, PartitionSpec as P

HEAD_DIM = 64
EPSILON = 1e-06
BF = jnp.bfloat16
F32 = jnp.float32
AXES = ("u", "z", "x")
PLANE = ("u", "x")


def dot_nn(a, b):
    return lax.dot_general(a, b, (((1,), (0,)), ((), ())), preferred_element_type=F32)


def dot_nt(a, b):
    return lax.dot_general(a, b, (((1,), (1,)), ((), ())), preferred_element_type=F32)


def dot_tn(a, b):
    return lax.dot_general(a, b, (((0,), (0,)), ((), ())), preferred_element_type=F32)


def attention_forward(q_ref, k_ref, v_ref, col_ref, row_ref, o_ref, lse_ref, acc, out_t):
    forward_heads(q_ref, k_ref, v_ref, col_ref, row_ref[...], o_ref, lse_ref, acc, out_t)


def forward_heads(q_ref, k_ref, v_ref, col_ref, segment_row, o_ref, lse_ref, acc, out_t):
    frames, width = q_ref.shape
    heads = width // HEAD_DIM
    block = frames // (frames // 352)
    lane = lax.broadcasted_iota(jnp.int32, (1, width), 1)
    for h in range(heads):
        own = (lane // HEAD_DIM == h).astype(BF)
        query = q_ref[...] * own
        acc[...] = jnp.zeros_like(acc)

        def step(j, carry):
            top, total = carry
            rows = pl.ds(pl.multiple_of(j * block, block), block)
            scores = dot_nt(k_ref[rows, :], query)
            scores = jnp.where(col_ref[rows, 0:1] == segment_row, scores, -1e30)
            peak = jnp.maximum(top, jnp.max(scores, axis=0, keepdims=True))
            expos = jnp.exp(scores - peak)
            shrink = jnp.exp(top - peak)
            acc[...] = acc[...] * shrink + dot_tn(v_ref[rows, :], expos.astype(BF))
            return peak, total * shrink + jnp.sum(expos, axis=0, keepdims=True)

        top, total = lax.fori_loop(
            0,
            frames // block,
            step,
            (jnp.full((1, frames), -1e30, F32), jnp.zeros((1, frames), F32)),
        )
        part = slice(h * HEAD_DIM, (h + 1) * HEAD_DIM)
        out_t[part, :] = acc[part, :] / total
        lse_ref[h : h + 1, :] = top + jnp.log(total)
    o_ref[...] = out_t[...].T.astype(BF)


def attention_backward(
    q_ref, k_ref, v_ref, o_ref, do_ref, col_ref, row_ref, lse_ref, dq_ref, dk_ref, dv_ref, acc
):
    backward_heads(
        q_ref, k_ref, v_ref, o_ref, do_ref, col_ref, row_ref[...], lse_ref, dq_ref, dk_ref, dv_ref, acc
    )


def backward_heads(
    q_ref, k_ref, v_ref, o_ref, do_ref, col_ref, segment_row, lse_ref, dq_ref, dk_ref, dv_ref, acc
):
    frames, width = q_ref.shape
    heads = width // HEAD_DIM
    block = frames // (frames // 352)
    lane = lax.broadcasted_iota(jnp.int32, (1, width), 1)
    product_t = (o_ref[...].astype(F32) * do_ref[...].astype(F32)).T
    for h in range(heads):
        own = (lane // HEAD_DIM == h).astype(BF)
        query = q_ref[...] * own
        grad = do_ref[...] * own
        part = slice(h * HEAD_DIM, (h + 1) * HEAD_DIM)
        delta = jnp.sum(product_t[part, :], axis=0, keepdims=True)
        log_total = lse_ref[h : h + 1, :]

        def step(j, _):
            rows = pl.ds(pl.multiple_of(j * block, block), block)
            keys = k_ref[rows, :]
            scores = dot_nt(keys, query)
            same = col_ref[rows, 0:1] == segment_row
            probs = jnp.where(same, jnp.exp(scores - log_total), 0.0)
            d_probs = dot_nt(v_ref[rows, :], grad)
            d_scores = (probs * (d_probs - delta)).astype(BF)
            value_part = dot_nn(probs.astype(BF), grad)
            key_part = dot_nn(d_scores, query)
            if h == 0:
                dv_ref[rows, :] = value_part
                dk_ref[rows, :] = key_part
            else:
                dv_ref[rows, :] += value_part
                dk_ref[rows, :] += key_part
            query_part = dot_tn(keys * own, d_scores)

            if h == 0:

                @pl.when(j == 0)
                def _():
                    acc[...] = query_part

                @pl.when(j > 0)
                def _():
                    acc[...] += query_part

            else:
                acc[...] += query_part
            return 0

        lax.fori_loop(0, frames // block, step, 0)
    dq_ref[...] = acc[...].T * (HEAD_DIM**-0.5)


def call_forward(query, keys, values, col, row):
    frames, width = query.shape
    return pl.pallas_call(
        attention_forward,
        out_shape=(
            jax.ShapeDtypeStruct((frames, width), BF),
            jax.ShapeDtypeStruct((width // HEAD_DIM, frames), F32),
        ),
        scratch_shapes=[pltpu.VMEM((width, frames), F32), pltpu.VMEM((width, frames), F32)],
        compiler_params=pltpu.CompilerParams(vmem_limit_bytes=56 * 2**20),
        cost_estimate=pl.CostEstimate(
            flops=16 * frames * frames * width, bytes_accessed=10 * frames * width, transcendentals=0
        ),
        name="attention_forward",
    )(query, keys, values, col, row)


def call_backward(query, keys, values, mixed, grad, col, row, lse):
    frames, width = query.shape
    shape = jax.ShapeDtypeStruct((frames, width), F32)
    return pl.pallas_call(
        attention_backward,
        out_shape=(shape, shape, shape),
        scratch_shapes=[pltpu.VMEM((width, frames), F32)],
        compiler_params=pltpu.CompilerParams(vmem_limit_bytes=56 * 2**20),
        cost_estimate=pl.CostEstimate(
            flops=32 * frames * frames * width, bytes_accessed=20 * frames * width, transcendentals=0
        ),
        name="attention_backward",
    )(query, keys, values, mixed, grad, col, row, lse)


def frame_segments(own_lengths, positions):
    slots = own_lengths.shape[0]
    upto = jnp.arange(slots)[:, None] >= jnp.arange(slots)[None, :]
    ends_at = jnp.sum(jnp.where(upto, own_lengths[None, :], 0), axis=1)
    starts_at = ends_at - own_lengths
    segment = jnp.sum((positions[:, None] >= ends_at[None, :]).astype(jnp.int32), axis=1)
    index = jnp.arange(slots, dtype=jnp.int32)
    offset = jnp.sum(jnp.where(segment[:, None] == index[None, :], starts_at[None, :], 0), axis=1)
    return segment, positions - offset


def rotary_tables(places):
    freqs = jnp.exp(
        jnp.arange(HEAD_DIM // 2, dtype=F32) * (-2.0 * math.log(10000.0) / HEAD_DIM)
    )
    angles = places.astype(F32)[:, None] * freqs[None, :]
    cosine, sine = jnp.cos(angles), jnp.sin(angles)
    return (
        jnp.concatenate([cosine, cosine], axis=1)[:, None, :],
        jnp.concatenate([-sine, sine], axis=1)[:, None, :],
    )


def rotate(v, tables, sign):
    frames, width = v.shape
    shaped = v.reshape(frames, width // HEAD_DIM, HEAD_DIM)
    half = HEAD_DIM // 2
    swapped = jnp.concatenate([shaped[..., half:], shaped[..., :half]], axis=-1)
    return (shaped * tables[0] + swapped * (sign * tables[1])).reshape(frames, width)


def rms_parts(hidden):
    return lax.rsqrt(jnp.mean(hidden * hidden, axis=-1, keepdims=True) + EPSILON)


def rms_back(hidden, inverse, gain, grad):
    scaled = hidden * inverse
    weighted = grad * gain
    inner = jnp.mean(weighted * scaled, axis=-1, keepdims=True)
    return inverse * (weighted - scaled * inner), jnp.sum(grad * scaled, axis=0)


def gelu_both(t):
    bell = 0.5 * (1.0 + lax.erf(t * 0.7071067811865476))
    return t * bell, bell + t * (0.3989422804014327 * jnp.exp(-0.5 * t * t))


TOK = 176
MESH_ID = pl.DeviceIdType.MESH


def flip_low(u):
    return u + 1 - 2 * lax.rem(u, 2)


def flip_high(u):
    return u + 2 - 4 * lax.div(u, 2)


def swap_bits(u):
    return 2 * lax.rem(u, 2) + lax.div(u, 2)


class Sender:
    def __init__(self, send, recv, load):
        self.send, self.recv, self.load = send, recv, load
        self.n = self.m = 0
        self.sent, self.kept = [], []

    def remote(self, src, dst, device, arrival=None):
        copy = pltpu.make_async_remote_copy(
            src_ref=src,
            dst_ref=dst,
            send_sem=self.send.at[self.n],
            recv_sem=self.recv.at[self.n] if arrival is None else arrival,
            device_id=device,
            device_id_type=MESH_ID,
        )
        self.n += 1
        return copy

    def push(self, src, dst, device):
        copy = self.remote(src, dst, device)
        copy.start()
        self.sent.append(copy)
        return copy

    def push_or_keep(self, src, dst, device, own, arrival=None):
        arrival = self.recv.at[self.n] if arrival is None else arrival
        inside = pltpu.make_async_copy(src, dst, arrival)
        copy = self.remote(src, dst, device, arrival)

        @pl.when(own)
        def _():
            inside.start()

        @pl.when(jnp.logical_not(own))
        def _():
            copy.start()

        self.kept.append((copy, own))
        return copy

    def local(self, src, dst):
        copy = pltpu.make_async_copy(src, dst, self.load.at[self.m])
        self.m += 1
        copy.start()
        return copy

    def finish(self):
        for copy in self.sent:
            copy.wait_send()
        for copy, own in self.kept:

            @pl.when(jnp.logical_not(own))
            def _(copy=copy):
                copy.wait_send()

        self.sent, self.kept = [], []


def plane_peers(u, z, x):
    peers = []
    for k in range(8):
        a = flip_low(u) if k & 2 else u
        a = flip_high(a) if k & 4 else a
        b = 1 - x if k & 1 else x
        peers.append(((a, z, b), 2 * a + b))
    return peers


def rows_of(p, start=0, size=TOK):
    return pl.ds(pl.multiple_of(p * TOK + start, 16), size)


def gather_blocks(sender, buffer, peers, use):
    me = peers[0][1]
    low, high = 80, 96

    def block(k, start=0, size=TOK):
        return buffer.at[rows_of(peers[k][1], start, size)]

    own_c = sender.push(block(0), block(0), peers[2][0])
    own_x = sender.push(block(0), block(0), peers[1][0])
    own_y = sender.push(block(0), block(0), peers[4][0])
    use(0)
    own_c.wait_recv()
    use(2)
    own_x.wait_recv()
    over_y = sender.push(block(1, low, high), block(1, low, high), peers[4][0])
    core_x = sender.push(block(1), block(1), peers[2][0])
    own_y.wait_recv()
    over_x = sender.push(block(4, 0, low), block(4, 0, low), peers[1][0])
    core_y = sender.push(block(4), block(4), peers[2][0])
    use(1)
    use(4)
    core_x.wait_recv()
    use(3)
    core_y.wait_recv()
    use(6)
    over_x.wait_recv()
    over_y.wait_recv()
    core_xy = sender.push(block(5), block(5), peers[2][0])
    use(5)
    core_xy.wait_recv()
    use(7)


def first_kernel(
    lens_ref,
    inputs_ref,
    skip_ref,
    cot_ref,
    w_skip_ref,
    w_qkv_ref,
    gain_ref,
    entry_out,
    cot_out,
    joined_out,
    normed_out,
    q_out,
    k_out,
    v_out,
    o_out,
    lse_out,
    cos_out,
    sin_out,
    seg_out,
    mixed_out,
    xin,
    xskip,
    wskip,
    wqkv,
    ent_send,
    jperm,
    cot_r,
    joined_r,
    lens_r,
    ent_r,
    n1,
    q,
    k,
    v,
    o,
    lse,
    cos_t,
    sin_t,
    seg_col,
    mixed,
    acc,
    out_t,
    send,
    recv,
    load,
    spread_recv,
):
    u, z, x = (lax.axis_index(a) for a in AXES)
    me = 2 * u + x
    peers = plane_peers(u, z, x)
    d = xin.shape[1]
    frames = n1.shape[0]
    plane = swap_bits(u)
    away = (z, plane, x)
    stays = jnp.logical_and(u == z, plane == z)
    sender = Sender(send, recv, load)

    got_x = sender.local(inputs_ref, xin)
    got_s = sender.local(skip_ref, xskip)
    got_w = sender.local(w_skip_ref, wskip)
    got_q = [
        sender.local(
            w_qkv_ref.at[:, pl.ds(pl.multiple_of(c * d + me * 128, 128), 128)],
            wqkv.at[:, pl.ds(c * 128, 128)],
        )
        for c in range(3)
    ]
    sent_lens = sender.push_or_keep(lens_ref, lens_r, away, stays)
    got_x.wait()
    got_s.wait()
    got_w.wait()
    sent_entry = []
    for n in range(2):
        part = slice(n * d // 2, (n + 1) * d // 2)
        value = dot_nn(xin[...], wskip[:d, part]) + dot_nn(xskip[...], wskip[d:, part])
        ent_send[:, part] = value.astype(BF)
        sent_entry.append(
            sender.push_or_keep(ent_send.at[:, part], ent_r.at[:, part], away, stays)
        )

    lane = lax.broadcasted_iota(jnp.int32, (TOK, 128), 1)
    for a in range(4):
        for b in range(2):
            for pair in range(2):
                halves = []
                for s in range(2):
                    block = 4 * (2 * pair + s) + 2 * b + a // 2
                    source = xin if block < d // 128 else xskip
                    first = block % (d // 128) * 128
                    piece = source[:, first : first + 128].astype(F32)
                    if a % 2 != s:
                        piece = pltpu.roll(piece, 64, 1)
                    halves.append(piece)
                place = (2 * a + b) * 256 + pair * 128
                jperm[:, place : place + 128] = jnp.where(lane < 64, halves[0], halves[1]).astype(BF)

    sent_lens.wait_recv()
    spread = lax.broadcasted_iota(jnp.int32, (TOK, 128), 1)
    freqs = jnp.exp(
        lax.rem(spread, 32).astype(F32) * (-2.0 * math.log(10000.0) / HEAD_DIM)
    )
    sign = jnp.where(lax.rem(spread, 64) < 32, -1.0, 1.0)
    slots = 6

    def table(i, _):
        rows = rows_of(i)
        at = (lax.broadcasted_iota(jnp.int32, (TOK, 128), 0) + i * TOK).astype(F32)
        place, segment, end = at, jnp.zeros_like(at), jnp.zeros((1, 128), F32)
        for s in range(slots):
            length = lens_r[s : s + 1, :]
            end = end + length
            past = at >= end
            segment = segment + jnp.where(past, 1.0, 0.0)
            place = place - jnp.where(past, length, 0.0)
        angle = place * freqs
        cos_t[rows, :] = jnp.cos(angle)
        sin_t[rows, :] = jnp.sin(angle) * sign
        seg_col[rows, :] = segment
        return 0

    lax.fori_loop(0, frames // TOK, table, 0)
    at = lax.broadcasted_iota(jnp.int32, (1, frames), 1).astype(F32)
    segment_row, end = jnp.zeros((1, frames), F32), jnp.zeros((1, 1), F32)
    for s in range(slots):
        end = end + lens_r[s : s + 1, 0:1]
        segment_row = segment_row + jnp.where(at >= end, 1.0, 0.0)

    for copy in sent_entry:
        copy.wait_recv()
    entry = ent_r[...].astype(F32)
    n1[rows_of(me), :] = (entry * rms_parts(entry) * gain_ref[...]).astype(BF)
    outs = [sender.local(ent_r, entry_out)]
    for copy in got_q:
        copy.wait()

    later = []

    def use(i):
        rows = rows_of(peers[i][1])
        value = dot_nn(n1[rows, :], wqkv[...])
        cosine, sine = cos_t[rows, :], sin_t[rows, :]
        front = lax.rem(lax.broadcasted_iota(jnp.int32, (TOK, 128), 1), 64) < 32

        def turn(t):
            swapped = jnp.where(front, pltpu.roll(t, 96, 1), pltpu.roll(t, 32, 1))
            return t * cosine + swapped * sine

        q[rows, :] = (turn(value[:, :128]).astype(BF).astype(F32) * HEAD_DIM**-0.5).astype(BF)
        k[rows, :] = turn(value[:, 128:256]).astype(BF)
        v[rows, :] = value[:, 256:].astype(BF)
        if i == 0:
            later.append(sender.push_or_keep(cot_ref, cot_r, away, stays))

    gather_blocks(sender, n1, peers, use)
    outs.append(sender.local(n1, normed_out))
    for a in range(4):
        for b in range(2):
            own = jnp.logical_and(jnp.logical_and(u == a, x == b), plane == z)
            sender.push_or_keep(
                jperm.at[:, pl.ds((2 * a + b) * 256, 256)],
                joined_r.at[rows_of(2 * z + x)],
                (a, plane, b),
                own,
                spread_recv.at[2 * z + x],
            )

    forward_heads(q, k, v, seg_col, segment_row, o, lse, acc, out_t)
    for src, dst in ((q, q_out), (k, k_out), (v, v_out), (o, o_out), (lse, lse_out)):
        outs.append(sender.local(src, dst))
    for src, dst in ((cos_t, cos_out), (sin_t, sin_out), (seg_col, seg_out)):
        outs.append(sender.local(src, dst))
    arrivals = [
        sender.push(
            o.at[rows_of(peers[i][1])],
            mixed.at[:, pl.ds(pl.multiple_of(me * 128, 128), 128)],
            peers[i][0],
        )
        for i in range(1, 8)
    ]
    own = sender.local(
        o.at[rows_of(me)], mixed.at[:, pl.ds(pl.multiple_of(me * 128, 128), 128)]
    )
    own.wait()
    for copy in arrivals:
        copy.wait_recv()
    outs.append(sender.local(mixed, mixed_out))
    for copy in later:
        copy.wait_recv()
    for s in range(8):
        rows = pl.ds(s * TOK, TOK)
        pltpu.make_async_copy(joined_r.at[rows], joined_r.at[rows], spread_recv.at[s]).wait()
    outs.append(sender.local(cot_r, cot_out))
    outs.append(sender.local(joined_r, joined_out))
    for copy in outs:
        copy.wait()
    sender.finish()


def call_first(lens, inputs, skip_in, cotangent, w_skip, w_qkv, gain_one):
    d = inputs.shape[1]
    group = 8 * TOK
    any_space = pl.BlockSpec(memory_space=pl.ANY)
    vmem = pl.BlockSpec(memory_space=pltpu.VMEM)
    wide, head, table = (group, d), ((group, 128), BF), ((group, 128), F32)
    outs = [
        ((TOK, d), BF),
        ((TOK, d), BF),
        ((group, 256), BF),
        (wide, BF),
        head,
        head,
        head,
        head,
        ((8, group), F32),
        table,
        table,
        table,
        ((TOK, d), BF),
    ]
    scratch = [
        ((TOK, d), BF),
        ((TOK, d), BF),
        ((2 * d, d), BF),
        ((d, 384), BF),
        ((TOK, d), BF),
        ((TOK, 2 * d), BF),
        ((TOK, d), BF),
        ((group, 256), BF),
        ((8, 128), F32),
        ((TOK, d), BF),
        (wide, BF),
        head,
        head,
        head,
        head,
        ((8, group), F32),
        table,
        table,
        table,
        ((TOK, d), BF),
        ((128, group), F32),
        ((128, group), F32),
    ]
    return pl.pallas_call(
        first_kernel,
        in_specs=[vmem] + [any_space] * 5 + [vmem],
        out_specs=[any_space] * len(outs),
        out_shape=[jax.ShapeDtypeStruct(*o) for o in outs],
        scratch_shapes=[pltpu.VMEM(*s) for s in scratch]
        + [pltpu.SemaphoreType.DMA((40,))] * 3
        + [pltpu.SemaphoreType.DMA((8,))],
        compiler_params=pltpu.CompilerParams(
            vmem_limit_bytes=56 * 2**20, has_side_effects=True
        ),
        name="entry_to_mixed",
    )(lens, inputs, skip_in, cotangent, w_skip, w_qkv, gain_one)


def local(
    sizes,
    inputs,
    skip_in,
    lengths,
    cotangent,
    w_skip,
    gain_one,
    w_qkv,
    w_out,
    gain_two,
    w_up,
    b_up,
    w_down,
    b_down,
):
    n_u, n_z, n_x = sizes
    frames, d = inputs.shape
    hidden = w_up.shape[1]
    parts = n_u * n_x
    group = frames * parts
    u, z, x = (lax.axis_index(a) for a in AXES)
    me = u * n_x + x
    width = d // parts

    def line(a, b, c):
        return (a * n_z + b) * n_x + c

    def permute(v, to):
        pairs = [
            (line(a, b, c), line(*to(a, b, c)))
            for a in range(n_u)
            for b in range(n_z)
            for c in range(n_x)
        ]
        return lax.ppermute(v, AXES, pairs)

    def plane_of(a):
        return (a % 2) * (n_u // 2) + a // 2

    group_of = {plane_of(a): a for a in range(n_u)}

    def away(v):
        return permute(v, lambda a, b, c: (b, plane_of(a), c))

    def home(v):
        return permute(v, lambda a, b, c: (group_of[b], a, c))

    def swap_plane(v, bit):
        def to(a, b, c):
            other = (a * n_x + c) ^ bit
            return other // n_x, b, other % n_x

        return permute(v, to)

    plane_bits = [1 << i for i in range(parts.bit_length() - 1)]
    if n_x == 2 and n_u == 4:
        orders = ([1, 4, 2], [4, 1, 2])
    else:
        orders = (plane_bits, plane_bits)
    cut = frames // 32 * 16

    def gather_plane(v):
        pieces = []
        for piece, order in zip((v[:cut], v[cut:]), orders):
            for bit in order:
                piece = jnp.concatenate([piece, swap_plane(piece, bit)], axis=0)
            pieces.append(piece)
        return jnp.concatenate(pieces, axis=0)

    def gather_order(v):
        pieces = []
        for start, size, order in ((0, cut, orders[0]), (cut, frames - cut, orders[1])):
            offsets = [0]
            for bit in order:
                offsets = offsets + [o ^ bit for o in offsets]
            for o in offsets:
                pieces.append(
                    lax.dynamic_slice_in_dim(v, (me ^ o) * frames + start, size, axis=0)
                )
        return jnp.concatenate(pieces, axis=0)

    z_bits = n_z.bit_length() - 1

    def reduce_z(v):
        rest = v.shape[1:]
        v = v.reshape((2,) * z_bits + (v.shape[0] // n_z,) + rest)
        for bit in range(z_bits):
            axis = z_bits - 1 - bit
            own = (z >> bit) & 1
            keep = lax.dynamic_index_in_dim(v, own, axis, keepdims=False)
            give = lax.dynamic_index_in_dim(v, 1 - own, axis, keepdims=False)
            got = permute(
                give.astype(BF), lambda a, b, c, bit=bit: (a, b ^ (1 << bit), c)
            )
            v = keep.astype(F32) + got.astype(F32)
            if bit < z_bits - 1:
                v = v.astype(BF)
        return v.astype(BF)

    def finish_columns(v):
        if n_x == 2:
            v = v.reshape((2, v.shape[0] // 2) + v.shape[1:])
            keep = lax.dynamic_index_in_dim(v, x, 0, keepdims=False)
            give = lax.dynamic_index_in_dim(v, 1 - x, 0, keepdims=False)
            got = permute(give, lambda a, b, c: (a, b, 1 - c))
            both = jnp.where(x == 0, jnp.stack([keep, got]), jnp.stack([got, keep]))
        else:
            both = v[None]
        every = lax.all_gather(both, "u", axis=0)
        return every.reshape((parts,) + both.shape[1:])

    def sum_all(v):
        total = n_u * n_z * n_x
        for i in range(total.bit_length() - 1):
            bit = 1 << i
            pairs = [(n, n ^ bit) for n in range(total)]
            v = v + lax.ppermute(v, AXES, pairs)
        return v

    entry_home = dot_nn(inputs, w_skip[:d]) + dot_nn(skip_in, w_skip[d:])
    entry = away(entry_home.astype(BF)).astype(F32)
    group_lengths = away(lengths)[0]
    grad_low = away(cotangent)
    inputs_away = away(inputs)
    skip_away = away(skip_in)

    segment, places = frame_segments(group_lengths, jnp.arange(group, dtype=jnp.int32))
    own_places = lax.dynamic_slice_in_dim(places, me * frames, frames)
    tables = rotary_tables(own_places)
    col, row = segment[:, None], segment[None, :]

    inverse_one = rms_parts(entry)
    normed_one = (entry * inverse_one * gain_one).astype(BF)
    qkv = dot_nn(normed_one, w_qkv)
    query = (rotate(qkv[:, :d], tables, 1.0)).astype(BF) * BF(HEAD_DIM**-0.5)
    keys = rotate(qkv[:, d : 2 * d], tables, 1.0).astype(BF)
    values = qkv[:, 2 * d :].astype(BF)

    def to_heads(*arrays):
        n = len(arrays)
        v = jnp.stack([a.reshape(frames, parts, width) for a in arrays], axis=2)
        v = lax.all_to_all(
            v.reshape(frames, parts * n * width), PLANE, split_axis=1, concat_axis=0, tiled=True
        )
        return [v[:, i * width : (i + 1) * width] for i in range(n)]

    def to_frames(*arrays):
        n = len(arrays)
        v = jnp.concatenate(arrays, axis=1)
        v = lax.all_to_all(v, PLANE, split_axis=0, concat_axis=1, tiled=True)
        v = v.reshape(frames, parts, n, width)
        return [v[:, :, i].reshape(frames, d) for i in range(n)]

    head_query, head_keys, head_values = to_heads(query, keys, values)
    head_mixed, lse = call_forward(head_query, head_keys, head_values, col, row)
    (mixed,) = to_frames(head_mixed)

    middle = entry + dot_nn(mixed, w_out)
    inverse_two = rms_parts(middle)
    normed_two = (middle * inverse_two * gain_two).astype(BF)
    up = dot_nn(normed_two, w_up) + b_up
    d_active = dot_nt(grad_low, w_down)
    active, slope = gelu_both(up)
    d_up = (d_active * slope).astype(BF)
    result_away = (middle + dot_nn(active.astype(BF), w_down) + b_down).astype(BF)
    result = home(result_away)
    d_normed_two = dot_nt(d_up, w_up)
    middle_part, g_gain_two = rms_back(middle, inverse_two, gain_two, d_normed_two)
    d_middle = grad_low.astype(F32) + middle_part
    d_branch = d_middle.astype(BF)
    d_mixed = dot_nt(d_branch, w_out).astype(BF)
    (head_grad,) = to_heads(d_mixed)
    dq, dk, dv = call_backward(
        head_query, head_keys, head_values, head_mixed, head_grad, col, row, lse
    )

    chunk = hidden // (n_z * parts)
    w_up_own = lax.dynamic_slice(
        w_up.reshape(d, n_z, n_x, n_u, chunk), (0, 0, x, u, 0), (d, n_z, 1, 1, chunk)
    ).reshape(d, n_z * chunk)
    w_down_own = lax.dynamic_slice(
        w_down.reshape(n_z, n_x, n_u, chunk, d), (0, x, u, 0, 0), (n_z, 1, 1, chunk, d)
    ).reshape(n_z * chunk, d)
    b_up_own = lax.dynamic_slice(
        b_up.reshape(n_z, n_x, n_u, chunk), (0, x, u, 0), (n_z, 1, 1, chunk)
    ).reshape(n_z * chunk)
    plane_grad = gather_plane(grad_low)
    plane_normed = gather_plane(normed_two)
    up_own = dot_nn(plane_normed, w_up_own) + b_up_own
    active_own, slope_own = gelu_both(up_own)
    d_up_own = (dot_nt(plane_grad, w_down_own) * slope_own).astype(BF)
    g_down = dot_tn(active_own.astype(BF), plane_grad)
    g_up = dot_tn(plane_normed, d_up_own)
    down_z = reduce_z(g_down.astype(BF))
    up_z = reduce_z(g_up.astype(BF))
    out_down = lax.all_gather(down_z, "u", axis=0, tiled=True).astype(F32)
    out_up = finish_columns(up_z)
    out_up = (
        out_up.reshape(n_u, n_x, -1, n_z, chunk).transpose(2, 3, 1, 0, 4).reshape(-1, hidden)
    ).astype(F32)

    plane_mixed = gather_plane(mixed)
    own_branch = gather_order(
        lax.all_to_all(d_branch, PLANE, split_axis=1, concat_axis=0, tiled=True)
    )
    g_out = dot_tn(plane_mixed, own_branch)
    out_out = (
        finish_columns(reduce_z(g_out.astype(BF))).transpose(1, 0, 2).reshape(-1, d).astype(F32)
    )

    low = [a.astype(BF) for a in (dq, dk, dv)]
    frame_query, frame_keys, frame_values = to_frames(*low)
    d_qkv = jnp.concatenate(
        [
            rotate(frame_query.astype(F32), tables, -1.0).astype(BF),
            rotate(frame_keys.astype(F32), tables, -1.0).astype(BF),
            frame_values,
        ],
        axis=1,
    )
    d_normed_one = dot_nt(d_qkv, w_qkv)
    entry_part, g_gain_one = rms_back(entry, inverse_one, gain_one, d_normed_one)
    d_entry = (d_middle + entry_part).astype(BF)
    d_entry_home = home(d_entry)
    d_joined = dot_nt(d_entry_home, w_skip)
    d_inputs = d_joined[:, :d].astype(BF)
    d_skip = d_joined[:, d:].astype(BF)

    group_tables = rotary_tables(places)
    head_d_qkv = jnp.concatenate(
        [
            rotate(low[0].astype(F32), group_tables, -1.0).astype(BF),
            rotate(low[1].astype(F32), group_tables, -1.0).astype(BF),
            low[2],
        ],
        axis=1,
    )
    plane_first = gather_plane(normed_one)
    g_qkv = dot_tn(plane_first, gather_order(head_d_qkv))
    plane_inputs = gather_plane(inputs_away)
    plane_skip = gather_plane(skip_away)
    own_entry = gather_order(
        lax.all_to_all(d_entry, PLANE, split_axis=1, concat_axis=0, tiled=True)
    )
    g_skip = jnp.concatenate([dot_tn(plane_inputs, own_entry), dot_tn(plane_skip, own_entry)])
    out_qkv = finish_columns(reduce_z(g_qkv.astype(BF)))
    out_qkv = (
        out_qkv.reshape(parts, -1, 3, width).transpose(1, 2, 0, 3).reshape(-1, 3 * d).astype(F32)
    )
    out_skip = (
        finish_columns(reduce_z(g_skip.astype(BF))).transpose(1, 0, 2).reshape(-1, d).astype(F32)
    )

    early = sum_all(
        jnp.concatenate(
            [
                g_gain_two,
                jnp.sum(d_up.astype(F32), axis=0),
                jnp.sum(cotangent.astype(F32), axis=0),
            ]
        )
    )
    total_gain_one = sum_all(g_gain_one)
    return (
        result,
        d_inputs,
        d_skip,
        out_skip,
        total_gain_one,
        out_qkv,
        out_out,
        early[:d],
        out_up,
        early[d : d + hidden],
        out_down,
        early[d + hidden :],
    )


def local_fast(
    sizes,
    inputs,
    skip_in,
    lengths,
    cotangent,
    w_skip,
    gain_one,
    w_qkv,
    w_out,
    gain_two,
    w_up,
    b_up,
    w_down,
    b_down,
):
    n_u, n_z, n_x = sizes
    frames, d = inputs.shape
    hidden = w_up.shape[1]
    parts = n_u * n_x
    group = frames * parts
    u, z, x = (lax.axis_index(a) for a in AXES)
    me = u * n_x + x
    width = d // parts

    def line(a, b, c):
        return (a * n_z + b) * n_x + c

    def permute(v, to):
        pairs = [
            (line(a, b, c), line(*to(a, b, c)))
            for a in range(n_u)
            for b in range(n_z)
            for c in range(n_x)
        ]
        return lax.ppermute(v, AXES, pairs)

    def plane_of(a):
        return (a % 2) * (n_u // 2) + a // 2

    group_of = {plane_of(a): a for a in range(n_u)}

    def away(v):
        return permute(v, lambda a, b, c: (b, plane_of(a), c))

    def home(v):
        return permute(v, lambda a, b, c: (group_of[b], a, c))

    def swap_plane(v, bit):
        def to(a, b, c):
            other = (a * n_x + c) ^ bit
            return other // n_x, b, other % n_x

        return permute(v, to)

    plane_bits = [1 << i for i in range(parts.bit_length() - 1)]
    if n_x == 2 and n_u == 4:
        orders = ([1, 4, 2], [4, 1, 2])
    else:
        orders = (plane_bits, plane_bits)
    cut = frames // 32 * 16

    def gather_plane(v):
        pieces = []
        for piece, order in zip((v[:cut], v[cut:]), orders):
            for bit in order:
                piece = jnp.concatenate([piece, swap_plane(piece, bit)], axis=0)
            pieces.append(piece)
        return jnp.concatenate(pieces, axis=0)

    def gather_order(v):
        pieces = []
        for start, size, order in ((0, cut, orders[0]), (cut, frames - cut, orders[1])):
            offsets = [0]
            for bit in order:
                offsets = offsets + [o ^ bit for o in offsets]
            for o in offsets:
                pieces.append(
                    lax.dynamic_slice_in_dim(v, (me ^ o) * frames + start, size, axis=0)
                )
        return jnp.concatenate(pieces, axis=0)

    z_bits = n_z.bit_length() - 1

    def reduce_z(v):
        rest = v.shape[1:]
        v = v.reshape((2,) * z_bits + (v.shape[0] // n_z,) + rest)
        for bit in range(z_bits):
            axis = z_bits - 1 - bit
            own = (z >> bit) & 1
            keep = lax.dynamic_index_in_dim(v, own, axis, keepdims=False)
            give = lax.dynamic_index_in_dim(v, 1 - own, axis, keepdims=False)
            got = permute(
                give.astype(BF), lambda a, b, c, bit=bit: (a, b ^ (1 << bit), c)
            )
            v = keep.astype(F32) + got.astype(F32)
            if bit < z_bits - 1:
                v = v.astype(BF)
        return v.astype(BF)

    def finish_columns(v):
        if n_x == 2:
            v = v.reshape((2, v.shape[0] // 2) + v.shape[1:])
            keep = lax.dynamic_index_in_dim(v, x, 0, keepdims=False)
            give = lax.dynamic_index_in_dim(v, 1 - x, 0, keepdims=False)
            got = permute(give, lambda a, b, c: (a, b, 1 - c))
            both = jnp.where(x == 0, jnp.stack([keep, got]), jnp.stack([got, keep]))
        else:
            both = v[None]
        every = lax.all_gather(both, "u", axis=0)
        return every.reshape((parts,) + both.shape[1:])

    def sum_all(v):
        total = n_u * n_z * n_x
        for i in range(total.bit_length() - 1):
            bit = 1 << i
            pairs = [(n, n ^ bit) for n in range(total)]
            v = v + lax.ppermute(v, AXES, pairs)
        return v

    lens = jnp.broadcast_to(
        jnp.pad(lengths[0].astype(F32), (0, 8 - lengths.shape[1]))[:, None], (8, 128)
    )
    (
        entry_low,
        grad_low,
        joined_own,
        plane_first,
        head_query,
        head_keys,
        head_values,
        head_mixed,
        lse8,
        cos_t,
        sin_t,
        seg_t,
        mixed,
    ) = call_first(lens, inputs, skip_in, cotangent, w_skip, w_qkv, gain_one[None])
    entry = entry_low.astype(F32)
    inverse_one = rms_parts(entry)
    lse = lse8[:2]
    col = seg_t[:, :1]
    row = col.reshape(1, group)
    own_cos = lax.dynamic_slice_in_dim(cos_t, me * frames, frames)[:, None, :64]
    own_sin = lax.dynamic_slice_in_dim(sin_t, me * frames, frames)[:, None, :64]
    tables = (own_cos, own_sin)
    group_tables = (cos_t[:, None, :64], sin_t[:, None, :64])
    def to_heads(*arrays):
        n = len(arrays)
        v = jnp.stack([a.reshape(frames, parts, width) for a in arrays], axis=2)
        v = lax.all_to_all(
            v.reshape(frames, parts * n * width), PLANE, split_axis=1, concat_axis=0, tiled=True
        )
        return [v[:, i * width : (i + 1) * width] for i in range(n)]

    def to_frames(*arrays):
        n = len(arrays)
        v = jnp.concatenate(arrays, axis=1)
        v = lax.all_to_all(v, PLANE, split_axis=0, concat_axis=1, tiled=True)
        v = v.reshape(frames, parts, n, width)
        return [v[:, :, i].reshape(frames, d) for i in range(n)]

    middle = entry + dot_nn(mixed, w_out)
    inverse_two = rms_parts(middle)
    normed_two = (middle * inverse_two * gain_two).astype(BF)
    up = dot_nn(normed_two, w_up) + b_up
    d_active = dot_nt(grad_low, w_down)
    active, slope = gelu_both(up)
    d_up = (d_active * slope).astype(BF)
    result_away = (middle + dot_nn(active.astype(BF), w_down) + b_down).astype(BF)
    result = home(result_away)
    d_normed_two = dot_nt(d_up, w_up)
    middle_part, g_gain_two = rms_back(middle, inverse_two, gain_two, d_normed_two)
    d_middle = grad_low.astype(F32) + middle_part
    d_branch = d_middle.astype(BF)
    d_mixed = dot_nt(d_branch, w_out).astype(BF)
    (head_grad,) = to_heads(d_mixed)
    dq, dk, dv = call_backward(
        head_query, head_keys, head_values, head_mixed, head_grad, col, row, lse
    )

    chunk = hidden // (n_z * parts)
    w_up_own = lax.dynamic_slice(
        w_up.reshape(d, n_z, n_x, n_u, chunk), (0, 0, x, u, 0), (d, n_z, 1, 1, chunk)
    ).reshape(d, n_z * chunk)
    w_down_own = lax.dynamic_slice(
        w_down.reshape(n_z, n_x, n_u, chunk, d), (0, x, u, 0, 0), (n_z, 1, 1, chunk, d)
    ).reshape(n_z * chunk, d)
    b_up_own = lax.dynamic_slice(
        b_up.reshape(n_z, n_x, n_u, chunk), (0, x, u, 0), (n_z, 1, 1, chunk)
    ).reshape(n_z * chunk)
    plane_grad = gather_plane(grad_low)
    plane_normed = gather_plane(normed_two)
    up_own = dot_nn(plane_normed, w_up_own) + b_up_own
    active_own, slope_own = gelu_both(up_own)
    d_up_own = (dot_nt(plane_grad, w_down_own) * slope_own).astype(BF)
    g_down = dot_tn(active_own.astype(BF), plane_grad)
    g_up = dot_tn(plane_normed, d_up_own)
    down_z = reduce_z(g_down.astype(BF))
    up_z = reduce_z(g_up.astype(BF))
    out_down = lax.all_gather(down_z, "u", axis=0, tiled=True).astype(F32)
    out_up = finish_columns(up_z)
    out_up = (
        out_up.reshape(n_u, n_x, -1, n_z, chunk).transpose(2, 3, 1, 0, 4).reshape(-1, hidden)
    ).astype(F32)

    plane_mixed = gather_plane(mixed)
    own_branch = gather_order(
        lax.all_to_all(d_branch, PLANE, split_axis=1, concat_axis=0, tiled=True)
    )
    g_out = dot_tn(plane_mixed, own_branch)
    out_out = (
        finish_columns(reduce_z(g_out.astype(BF))).transpose(1, 0, 2).reshape(-1, d).astype(F32)
    )

    low = [a.astype(BF) for a in (dq, dk, dv)]
    frame_query, frame_keys, frame_values = to_frames(*low)
    d_qkv = jnp.concatenate(
        [
            rotate(frame_query.astype(F32), tables, -1.0).astype(BF),
            rotate(frame_keys.astype(F32), tables, -1.0).astype(BF),
            frame_values,
        ],
        axis=1,
    )
    d_normed_one = dot_nt(d_qkv, w_qkv)
    entry_part, g_gain_one = rms_back(entry, inverse_one, gain_one, d_normed_one)
    d_entry = (d_middle + entry_part).astype(BF)
    d_entry_home = home(d_entry)
    d_joined = dot_nt(d_entry_home, w_skip)
    d_inputs = d_joined[:, :d].astype(BF)
    d_skip = d_joined[:, d:].astype(BF)

    head_d_qkv = jnp.concatenate(
        [
            rotate(low[0].astype(F32), group_tables, -1.0).astype(BF),
            rotate(low[1].astype(F32), group_tables, -1.0).astype(BF),
            low[2],
        ],
        axis=1,
    )
    g_qkv = dot_tn(plane_first, head_d_qkv)
    g_skip = dot_tn(joined_own, lax.all_gather(d_entry, PLANE, axis=0, tiled=True))
    out_qkv = finish_columns(reduce_z(g_qkv.astype(BF)))
    out_qkv = (
        out_qkv.reshape(parts, -1, 3, width).transpose(1, 2, 0, 3).reshape(-1, 3 * d).astype(F32)
    )
    out_skip = lax.all_gather(
        reduce_z(g_skip.astype(BF)), "u", axis=0, tiled=True
    ).astype(F32)

    early = sum_all(
        jnp.concatenate(
            [
                g_gain_two,
                jnp.sum(d_up.astype(F32), axis=0),
                jnp.sum(cotangent.astype(F32), axis=0),
            ]
        )
    )
    total_gain_one = sum_all(g_gain_one)
    return (
        result,
        d_inputs,
        d_skip,
        out_skip,
        total_gain_one,
        out_qkv,
        out_out,
        early[:d],
        out_up,
        early[d : d + hidden],
        out_down,
        early[d + hidden :],
    )


def solution(mesh):
    n_u, n_s = mesh.shape["utt"], mesh.shape["seq"]
    sizes = (n_u, n_u, n_s // n_u)
    program = local_fast if sizes == (4, 4, 2) else local
    inner = Mesh(mesh.devices.reshape(sizes), AXES)
    rows, seq = P(AXES, None), P(("z", "x"), None)
    in_specs = (rows, rows, P("u", None), rows) + (P(),) * 9
    out_specs = (rows, rows, rows, seq, P(), seq, seq, P(), seq, P(), seq, P())
    return jax.shard_map(
        functools.partial(program, sizes),
        mesh=inner,
        in_specs=in_specs,
        out_specs=out_specs,
        check_vma=False,
    )
```

profile of v0, /device:TPU:5, one launch (start us, length us, event | category | flops | bytes accessed | tf_op | source)
XLA Modules:
  0.0 469.4 jit_solution(16121271625315285514)
XLA Ops:
  8.7 76.3 %entry_to_mixed.1 = (bf16[176,1024]{1,0:T(8,128)(2,1)}, bf16[176,1024]{1,0:T(8,128)(2,1)}, bf16[1408,256]{1,0:T(8,128)(2,1)}, bf16[1408,1024]{1,0:T(8,128)(2,1)}...) custom-call(f32[8,128]{1,0:T(8,128)} %broadcast_in_dim.4.lens_ref, ...), custom_call_target="tpu_custom_call" | custom-call | tf_op jit(solution)/shard_map/entry_to_mixed/pallas_call | solution.py:572
  87.2 5.2 %convolution_add_fusion = f32[176,4096]{1,0:T(8,128)S(1)} fusion(bf16[176,1024]{1,0:T(8,128)(2,1)S(1)} %multiply_convert_fusion.10, bf16[1024,4096]{1,0:T(8,128)(2,1)} %param.22, f32[4096]{0:T(1024)S(1)} %copy-done.28), kind=kOutput, calls=%fused_computation.1 | convolution fusion | flops 1477115904 | bytes 11649024 | tf_op jit(solution)/shard_map/dot_general | solution.py:20
  92.5 4.5 convert_reduce_fusion
  97.0 5.1 %multiply_reduce_fusion = (f32[1024]{0:T(1024)}, f32[176]{0:T(256)S(1)}, f32[176,1024]{1,0:T(8,128)S(1)}) fusion(f32[176,1024]{1,0:T(8,128)S(1)} %get-tuple-element.130, f32[176]{0:T(256)S(1)} %add_rsqrt_fusion.1, f32[1024]{0:T(1024)S(1)} %copy-done.30, bf16[176,4096]{1,0:T(8,128)(2,1)} %get-tuple-element.134, bf16[1024,4096]{1,0:T(8,128)(2,1)S(1)} %bitcast.188), kind=kOutput, calls=%fused_computation.80 | convolution fusion | flops 1477475200 | bytes 11281792 | tf_op jit(solution)/shard_map/dot_general | solution.py:24
  103.1 5.9 %all-to-all-start.2 = ((bf16[176,8,128]{2,0,1:T(8,128)(2,1)}), bf16[176,8,128]{2,0,1:T(8,128)(2,1)}, u32[]{:S(2)}, u32[]{:S(2)}) async-start(bf16[176,8,128]{2,0,1:T(8,128)(2,1)} %bitcast.208), calls=%async_computation.2 | async-start | bytes 720896 | tf_op jit(solution)/shard_map/all_to_all | solution.py:1075
  113.2 6.6 %fusion.13 = bf16[176,1024]{1,0:T(8,128)(2,1)} fusion(f32[176,1024]{1,0:T(8,128)S(1)} %get-tuple-element.130, bf16[4096,1024]{1,0:T(8,128)(2,1)} %param.24, f32[176,4096]{1,0:T(8,128)} %copy-done.6, f32[1024]{0:T(1024)} %param.25), kind=kOutput, calls=%fused_computation.35 | convolution fusion | flops 1480540160 | bytes 12357632 | tf_op jit(solution)/shard_map/dot_general | solution.py:20
  119.9 2.3 collective-permute-start
  133.7 2.3 constant_dynamic-slice_fusion.2
  136.0 12.0 %copy.139 = bf16[1024,4096]{0,1:T(8,128)(2,1)} copy(bf16[1024,4096]{1,0:T(8,128)(2,1)} %param.22) | data formatting | bytes 16777216 | tf_op args[9]
  149.8 2.3 constant_dynamic-slice_fusion.1
  152.2 3.5 collective-permute-start.24
  174.5 6.1 %all-to-all-start = ((bf16[176,8,128]{2,0,1:T(8,128)(2,1)}), bf16[176,8,128]{2,0,1:T(8,128)(2,1)S(1)}, u32[]{:S(2)}, u32[]{:S(2)}) async-start(bf16[176,8,128]{2,0,1:T(8,128)(2,1)} %bitcast.185), calls=%async_computation | async-start | bytes 720896 | tf_op jit(solution)/shard_map/all_to_all | solution.py:1017
  185.1 9.9 %all-to-all-done = bf16[176,8,128]{2,0,1:T(8,128)(2,1)S(1)} async-done(((bf16[176,8,128]{2,0,1:T(8,128)(2,1)}), bf16[176,8,128]{2,0,1:T(8,128)(2,1)S(1)}, u32[]{:S(2)}, u32[]{:S(2)}) %all-to-all-start) | async-done | bytes 360480 | tf_op jit(solution)/shard_map/all_to_all | solution.py:1017
  195.7 15.6 %attention_backward.1 = (f32[1408,128]{1,0:T(8,128)}, f32[1408,128]{1,0:T(8,128)}, f32[1408,128]{1,0:T(8,128)}) custom-call(bf16[1408,128]{1,0:T(8,128)(2,1)} %get-tuple-element.31.q_ref, bf16[1408,128]{1,0:T(8,128)(2,1)} %get-tuple-element.32.k_ref, bf16[1408,128]{1,0:T(8,128)(2,1)} %get-tuple-element.33.v_ref, bf16[1408,128]{1,0:T(8,128)(2,1)} %get-tuple-element.34.o_ref, ...), custom_call_target="tpu_custom_call" | custom-call | flops 8120172544 | bytes 3604480 | tf_op jit(solution)/shard_map/attention_backward/pallas_call | solution.py:148
  218.1 5.0 %all-to-all-start.1 = ((bf16[8,176,384]{2,1,0:T(8,128)(2,1)}), bf16[8,176,384]{2,1,0:T(8,128)(2,1)S(1)}, u32[]{:S(2)}, u32[]{:S(2)}) async-start(bf16[8,176,384]{2,1,0:T(8,128)(2,1)} %bitcast.194), calls=%async_computation.1 | async-start | bytes 2162688 | tf_op jit(solution)/shard_map/all_to_all | solution.py:1025
  226.3 2.3 copy.131
  228.6 2.2 copy.134
  230.8 2.1 add_convert_fusion.1
  256.9 8.1 %collective-permute-done.10 = bf16[256,384]{1,0:T(8,128)(2,1)S(1)} collective-permute-done((bf16[256,384]{1,0:T(8,128)(2,1)S(1)}, bf16[256,384]{1,0:T(8,128)(2,1)S(1)}, u32[]{:S(2)}, u32[]{:S(2)}) %collective-permute-start.10) | collective-permute-done | bytes 196640 | tf_op jit(solution)/shard_map/ppermute | solution.py:902
  282.7 2.4 copy.121
  285.1 2.4 copy.124
  289.4 5.2 %fusion.35 = (f32[1024]{0:T(1024)S(1)}, f32[176]{0:T(256)S(1)}, f32[176,1024]{1,0:T(8,128)S(1)}) fusion(bf16[176,1024]{1,0:T(8,128)(2,1)S(1)} %copy-done.5, f32[176]{0:T(256)S(1)} %copy-done.31, f32[1024]{0:T(1024)S(1)} %copy-done.29, bf16[1024,3072]{1,0:T(8,128)(2,1)} %w_qkv_ref.1, bf16[176,1024]{1,0:T(8,128)(2,1)S(1)} %bitcast.223, ...), kind=kOutput, calls=%fused_computation.69 | convolution fusion | flops 1111800704 | bytes 8463744 | tf_op jit(solution)/shard_map/dot_general | solution.py:24
  297.2 2.6 collective-permute-done.5
  300.8 2.3 collective-permute-done.6
  303.1 5.2 %collective-permute-start.7 = (f32[1024]{0:T(1024)S(1)}, f32[1024]{0:T(1024)S(1)}, u32[]{:S(2)}, u32[]{:S(2)}) collective-permute-start(f32[1024]{0:T(1024)S(1)} %add.330), channel_id=1, source_target_pairs={{0,8},{1,9},{2,10},{3,11},{4,12},{5,13},{6,14},{7,15},{8,0},{9,1},... | collective-permute-start | bytes 12296 | tf_op jit(solution)/shard_map/ppermute | solution.py:984
  312.3 11.1 %all_gather.23 = bf16[4,2,128,384]{3,2,1,0:T(8,128)(2,1)S(1)} all-gather(bf16[1,2,128,384]{3,2,1,0:T(8,128)(2,1)S(1)} %copy-done.22), channel_id=1, replica_groups=mesh['u'=4,'z'=4,'x'=2] {'u'}, dimensions={0}, use_global_device_ids=true | all-gather | bytes 983040 | tf_op jit(solution)/shard_map/all_gather | solution.py:976
  328.3 2.2 pad_maximum_fusion.4
  331.1 4.8 %collective-permute-done.36 = bf16[192,1024]{1,0:T(8,128)(2,1)S(1)} collective-permute-done((bf16[192,1024]{1,0:T(8,128)(2,1)}, bf16[192,1024]{1,0:T(8,128)(2,1)S(1)}, u32[]{:S(2)}, u32[]{:S(2)}) %collective-permute-start.36) | collective-permute-done | bytes 393248 | tf_op jit(solution)/shard_map/ppermute | solution.py:902
  340.3 3.1 copy.143
  343.4 2.1 collective-permute-start.1
  353.0 2.1 constant_dynamic-update-slice_fusion.24
  355.1 2.1 constant_dynamic-update-slice_fusion.32
  357.2 3.5 convolution_add_fusion.1
  360.7 5.0 %convolution_convert_fusion.1 = bf16[512,1024]{1,0:T(8,128)(2,1)S(1)} fusion(bf16[1408,1024]{1,0:T(8,128)(2,1)} %constant_dynamic-update-slice_fusion.32, f32[1408,512]{1,0:T(8,128)S(1)} %convolution_add_fusion.1), kind=kOutput, calls=%fused_computation.24 | convolution fusion | flops 1480523776 | bytes 6815744 | tf_op jit(solution)/shard_map/dot_general | solution.py:28
  366.8 8.4 %convolution_convert_fusion.2 = bf16[1024,512]{1,0:T(8,128)(2,1)} fusion(bf16[1408,1024]{1,0:T(8,128)(2,1)} %constant_dynamic-update-slice_fusion.24, bf16[1408,1024]{1,0:T(8,128)(2,1)} %constant_dynamic-update-slice_fusion.32, bf16[512,1024]{1,0:T(8,128)(2,1)} %bitcast.214, f32[1408,512]{1,0:T(8,128)} %copy-done.36), kind=kOutput, calls=%fused_computation.25 | convolution fusion | flops 2960523264 | bytes 10747904 | tf_op jit(solution)/shard_map/dot_general | solution.py:28
  384.6 2.1 constant_dynamic-update-slice_fusion
  386.7 8.7 %collective-permute-done.42 = bf16[128,1024]{1,0:T(8,128)(2,1)S(1)} collective-permute-done((bf16[128,1024]{1,0:T(8,128)(2,1)S(1)}, bf16[128,1024]{1,0:T(8,128)(2,1)S(1)}, u32[]{:S(2)}, u32[]{:S(2)}) %collective-permute-start.42) | collective-permute-done | bytes 262176 | tf_op jit(solution)/shard_map/ppermute | solution.py:902
  398.4 2.2 collective-permute-start.39
  400.6 2.8 convolution_convert_fusion.6
  403.6 8.6 %collective-permute-done.39 = bf16[256,512]{1,0:T(8,128)(2,1)S(1)} collective-permute-done((bf16[256,512]{1,0:T(8,128)(2,1)S(1)}, bf16[256,512]{1,0:T(8,128)(2,1)S(1)}, u32[]{:S(2)}, u32[]{:S(2)}) %collective-permute-start.39) | collective-permute-done | bytes 262176 | tf_op jit(solution)/shard_map/ppermute | solution.py:902
  413.6 2.5 collective-permute-done.40
  416.9 3.9 convolution_convert_fusion
  423.7 2.8 convolution_convert_fusion.4
  426.7 10.0 %all_gather.24 = bf16[4,2,128,128]{3,2,1,0:T(8,128)(2,1)S(1)} all-gather(bf16[1,2,128,128]{3,2,1,0:T(8,128)(2,1)S(1)} %maximum_select_fusion.2), channel_id=1, replica_groups=mesh['u'=4,'z'=4,'x'=2] {'u'}, dimensions={0}, use_global_device_ids=true | all-gather | bytes 327680 | tf_op jit(solution)/shard_map/all_gather | solution.py:976
  437.6 2.8 convert_element_type.369
  442.7 2.4 collective-permute-start.3
  446.9 3.0 copy.144
  451.8 8.0 %all_gather.22 = bf16[256,1024]{1,0:T(8,128)(2,1)S(1)} all-gather(bf16[64,1024]{1,0:T(8,128)(2,1)S(1)} %fusion.46), channel_id=1, replica_groups=mesh['u'=4,'z'=4,'x'=2] {'u'}, dimensions={0}, use_global_device_ids=true | all-gather | bytes 655360 | tf_op jit(solution)/shard_map/all_gather | solution.py:1114
  (312 shorter events, 152.9 us)
Async XLA Ops:
  103.1 71.4 %all-to-all-start.2 = ((bf16[176,8,128]{2,0,1:T(8,128)(2,1)}), bf16[176,8,128]{2,0,1:T(8,128)(2,1)}, u32[]{:S(2)}, u32[]{:S(2)}) async-start(bf16[176,8,128]{2,0,1:T(8,128)(2,1)} %bitcast.208), calls=%async_computation.2 | async-start | bytes 720896 | tf_op jit(solution)/shard_map/all_to_all | solution.py:1075
  112.0 21.0 %collective-permute-start.21 = (f32[6144]{0:T(1024)}, f32[6144]{0:T(1024)}, u32[]{:S(2)}, u32[]{:S(2)}) collective-permute-start(f32[6144]{0:T(1024)} %pad_maximum_fusion.15), channel_id=1, source_target_pairs={{0,1},{1,0},{2,3},{3,2},{4,5},{5,4},{6,7},{7,6},{8,9},{9,8},{10,11... | collective-permute-start | bytes 73736 | tf_op jit(solution)/shard_map/ppermute | solution.py:984
  119.9 128.0 %collective-permute-start = (bf16[176,1024]{1,0:T(8,128)(2,1)}, bf16[176,1024]{1,0:T(8,128)(2,1)}, u32[]{:S(2)}, u32[]{:S(2)}) collective-permute-start(bf16[176,1024]{1,0:T(8,128)(2,1)} %fusion.13), channel_id=1, source_target_pairs={{0,0},{1,1},{2,16},{3,17},{4,8},{5,9},{6,24},{7,25},{8,2},{9,3},{1... | collective-permute-start | bytes 1081352 | tf_op jit(solution)/shard_map/ppermute | solution.py:902
  123.8 42.3 %collective-permute-start.26 = (bf16[80,1024]{1,0:T(8,128)(2,1)}, bf16[80,1024]{1,0:T(8,128)(2,1)}, u32[]{:S(2)}, u32[]{:S(2)}) collective-permute-start(bf16[80,1024]{1,0:T(8,128)(2,1)} %get-tuple-element.111), channel_id=1, source_target_pairs={{0,1},{1,0},{2,3},{3,2},{4,5},{5,4},{6,7},{7,6},{8,9},{9,8},{10,11... | collective-permute-start | bytes 491528 | tf_op jit(solution)/shard_map/ppermute | solution.py:902
  125.8 42.2 %collective-permute-start.12 = (bf16[80,1024]{1,0:T(8,128)(2,1)}, bf16[80,1024]{1,0:T(8,128)(2,1)}, u32[]{:S(2)}, u32[]{:S(2)}) collective-permute-start(bf16[80,1024]{1,0:T(8,128)(2,1)} %get-tuple-element.115), channel_id=1, source_target_pairs={{0,1},{1,0},{2,3},{3,2},{4,5},{5,4},{6,7},{7,6},{8,9},{9,8},{10,11... | collective-permute-start | bytes 491528 | tf_op jit(solution)/shard_map/ppermute | solution.py:902
  128.7 42.5 %collective-permute-start.32 = (bf16[80,1024]{1,0:T(8,128)(2,1)}, bf16[80,1024]{1,0:T(8,128)(2,1)}, u32[]{:S(2)}, u32[]{:S(2)}) collective-permute-start(bf16[80,1024]{1,0:T(8,128)(2,1)} %get-tuple-element.107), channel_id=1, source_target_pairs={{0,1},{1,0},{2,3},{3,2},{4,5},{5,4},{6,7},{7,6},{8,9},{9,8},{10,11... | collective-permute-start | bytes 491528 | tf_op jit(solution)/shard_map/ppermute | solution.py:902
  133.7 14.3 %collective-permute-start.22 = (f32[6144]{0:T(1024)S(1)}, f32[6144]{0:T(1024)S(1)}, u32[]{:S(2)}, u32[]{:S(2)}) collective-permute-start(f32[6144]{0:T(1024)S(1)} %fusion.53), channel_id=1, source_target_pairs={{0,2},{1,3},{2,0},{3,1},{4,6},{5,7},{6,4},{7,5},{8,10},{9,11},{10,... | collective-permute-start | bytes 73736 | tf_op jit(solution)/shard_map/ppermute | solution.py:984
  148.0 4.2 collective-permute-start.23
  152.2 4.4 collective-permute-start.24
  156.6 8.3 %collective-permute-start.25 = (f32[6144]{0:T(1024)S(1)}, f32[6144]{0:T(1024)S(1)}, u32[]{:S(2)}, u32[]{:S(2)}) collective-permute-start(f32[6144]{0:T(1024)S(1)} %add.367), channel_id=1, source_target_pairs={{0,16},{1,17},{2,18},{3,19},{4,20},{5,21},{6,22},{7,23},{8,24},{9,... | collective-permute-start | bytes 73736 | tf_op jit(solution)/shard_map/ppermute | solution.py:984
  167.9 80.0 %collective-permute-start.27 = (bf16[160,1024]{1,0:T(8,128)(2,1)}, bf16[160,1024]{1,0:T(8,128)(2,1)}, u32[]{:S(2)}, u32[]{:S(2)}) collective-permute-start(bf16[160,1024]{1,0:T(8,128)(2,1)} %pad_maximum_fusion.13), channel_id=1, source_target_pairs={{0,16},{1,17},{2,18},{3,19},{4,20},{5,21},{6,22},{7,23},{8,24},{9,... | collective-permute-start | bytes 983048 | tf_op jit(solution)/shard_map/ppermute | solution.py:902
  169.7 80.2 %collective-permute-start.13 = (bf16[160,1024]{1,0:T(8,128)(2,1)}, bf16[160,1024]{1,0:T(8,128)(2,1)}, u32[]{:S(2)}, u32[]{:S(2)}) collective-permute-start(bf16[160,1024]{1,0:T(8,128)(2,1)} %pad_maximum_fusion.12), channel_id=1, source_target_pairs={{0,16},{1,17},{2,18},{3,19},{4,20},{5,21},{6,22},{7,23},{8,24},{9,... | collective-permute-start | bytes 983048 | tf_op jit(solution)/shard_map/ppermute | solution.py:902
  172.9 78.2 %collective-permute-start.33 = (bf16[160,1024]{1,0:T(8,128)(2,1)}, bf16[160,1024]{1,0:T(8,128)(2,1)}, u32[]{:S(2)}, u32[]{:S(2)}) collective-permute-start(bf16[160,1024]{1,0:T(8,128)(2,1)} %pad_maximum_fusion.14), channel_id=1, source_target_pairs={{0,16},{1,17},{2,18},{3,19},{4,20},{5,21},{6,22},{7,23},{8,24},{9,... | collective-permute-start | bytes 983048 | tf_op jit(solution)/shard_map/ppermute | solution.py:902
  174.5 20.5 %all-to-all-start = ((bf16[176,8,128]{2,0,1:T(8,128)(2,1)}), bf16[176,8,128]{2,0,1:T(8,128)(2,1)S(1)}, u32[]{:S(2)}, u32[]{:S(2)}) async-start(bf16[176,8,128]{2,0,1:T(8,128)(2,1)} %bitcast.185), calls=%async_computation | async-start | bytes 720896 | tf_op jit(solution)/shard_map/all_to_all | solution.py:1017
  218.1 57.4 %all-to-all-start.1 = ((bf16[8,176,384]{2,1,0:T(8,128)(2,1)}), bf16[8,176,384]{2,1,0:T(8,128)(2,1)S(1)}, u32[]{:S(2)}, u32[]{:S(2)}) async-start(bf16[8,176,384]{2,1,0:T(8,128)(2,1)} %bitcast.194), calls=%async_computation.1 | async-start | bytes 2162688 | tf_op jit(solution)/shard_map/all_to_all | solution.py:1025
  223.1 200.6 %all-gather.4.cloned.1.call-start = ((), (), s32[]{:S(2)}) async-start(), calls=%async_computation.3 | async-start | bytes 3244032 | tf_op jit(solution)/shard_map/all_gather | solution.py:1109
  235.4 17.4 %collective-permute-start.9 = (bf16[2,256,384]{2,1,0:T(8,128)(2,1)S(1)}, bf16[2,256,384]{2,1,0:T(8,128)(2,1)S(1)}, u32[]{:S(2)}, u32[]{:S(2)}) collective-permute-start(bf16[2,256,384]{2,1,0:T(8,128)(2,1)S(1)} %dynamic-slice_bitcast_fusion.2), channel_id=1, source_target_pairs={{0,2},{1,3},{2,0},{3,1},{4,6},{5,7},{6,4},{7,5},{8,10},{9,11},{10,... | collective-permute-start | bytes 1179656 | tf_op jit(solution)/shard_map/ppermute | solution.py:902
  249.2 20.6 %collective-permute-start.28 = (bf16[320,1024]{1,0:T(8,128)(2,1)S(1)}, bf16[320,1024]{1,0:T(8,128)(2,1)S(1)}, u32[]{:S(2)}, u32[]{:S(2)}) collective-permute-start(bf16[320,1024]{1,0:T(8,128)(2,1)S(1)} %pad_maximum_fusion.7), channel_id=1, source_target_pairs={{0,8},{1,9},{2,10},{3,11},{4,12},{5,13},{6,14},{7,15},{8,0},{9,1},... | collective-permute-start | bytes 1966088 | tf_op jit(solution)/shard_map/ppermute | solution.py:902
  251.0 20.7 %collective-permute-start.14 = (bf16[320,1024]{1,0:T(8,128)(2,1)S(1)}, bf16[320,1024]{1,0:T(8,128)(2,1)S(1)}, u32[]{:S(2)}, u32[]{:S(2)}) collective-permute-start(bf16[320,1024]{1,0:T(8,128)(2,1)S(1)} %pad_maximum_fusion.6), channel_id=1, source_target_pairs={{0,8},{1,9},{2,10},{3,11},{4,12},{5,13},{6,14},{7,15},{8,0},{9,1},... | collective-permute-start | bytes 1966088 | tf_op jit(solution)/shard_map/ppermute | solution.py:902
  252.3 22.3 %collective-permute-start.34 = (bf16[320,1024]{1,0:T(8,128)(2,1)S(1)}, bf16[320,1024]{1,0:T(8,128)(2,1)S(1)}, u32[]{:S(2)}, u32[]{:S(2)}) collective-permute-start(bf16[320,1024]{1,0:T(8,128)(2,1)S(1)} %pad_maximum_fusion.8), channel_id=1, source_target_pairs={{0,8},{1,9},{2,10},{3,11},{4,12},{5,13},{6,14},{7,15},{8,0},{9,1},... | collective-permute-start | bytes 1966088 | tf_op jit(solution)/shard_map/ppermute | solution.py:902
  253.0 12.0 %collective-permute-start.10 = (bf16[256,384]{1,0:T(8,128)(2,1)S(1)}, bf16[256,384]{1,0:T(8,128)(2,1)S(1)}, u32[]{:S(2)}, u32[]{:S(2)}) collective-permute-start(bf16[256,384]{1,0:T(8,128)(2,1)S(1)} %dynamic-slice_bitcast_fusion.6), channel_id=1, source_target_pairs={{0,4},{1,5},{2,6},{3,7},{4,0},{5,1},{6,2},{7,3},{8,12},{9,13},{10,... | collective-permute-start | bytes 589832 | tf_op jit(solution)/shard_map/ppermute | solution.py:902
  265.0 4.0 collective-permute-start.11
  271.4 36.9 %collective-permute-start.29 = (bf16[96,1024]{1,0:T(8,128)(2,1)}, bf16[96,1024]{1,0:T(8,128)(2,1)}, u32[]{:S(2)}, u32[]{:S(2)}) collective-permute-start(bf16[96,1024]{1,0:T(8,128)(2,1)} %get-tuple-element.109), channel_id=1, source_target_pairs={{0,16},{1,17},{2,18},{3,19},{4,20},{5,21},{6,22},{7,23},{8,24},{9,... | collective-permute-start | bytes 589832 | tf_op jit(solution)/shard_map/ppermute | solution.py:902
  273.4 51.9 %collective-permute-start.15 = (bf16[96,1024]{1,0:T(8,128)(2,1)}, bf16[96,1024]{1,0:T(8,128)(2,1)}, u32[]{:S(2)}, u32[]{:S(2)}) collective-permute-start(bf16[96,1024]{1,0:T(8,128)(2,1)} %get-tuple-element.113), channel_id=1, source_target_pairs={{0,16},{1,17},{2,18},{3,19},{4,20},{5,21},{6,22},{7,23},{8,24},{9,... | collective-permute-start | bytes 589832 | tf_op jit(solution)/shard_map/ppermute | solution.py:902
  296.6 14.7 %collective-permute-start.35 = (bf16[96,1024]{1,0:T(8,128)(2,1)S(1)}, bf16[96,1024]{1,0:T(8,128)(2,1)S(1)}, u32[]{:S(2)}, u32[]{:S(2)}) collective-permute-start(bf16[96,1024]{1,0:T(8,128)(2,1)S(1)} %get-tuple-element.105), channel_id=1, source_target_pairs={{0,16},{1,17},{2,18},{3,19},{4,20},{5,21},{6,22},{7,23},{8,24},{9,... | collective-permute-start | bytes 589832 | tf_op jit(solution)/shard_map/ppermute | solution.py:902
  297.2 2.6 collective-permute-start.5
  299.8 3.4 collective-permute-start.6
  300.8 136.8 %all-gather.8.cloned.1.call-start = ((), (), s32[]{:S(2)}) async-start(), calls=%async_computation.5 | async-start | bytes 1310720 | tf_op jit(solution)/shard_map/all_gather | solution.py:1067
  303.1 20.7 %collective-permute-start.7 = (f32[1024]{0:T(1024)S(1)}, f32[1024]{0:T(1024)S(1)}, u32[]{:S(2)}, u32[]{:S(2)}) collective-permute-start(f32[1024]{0:T(1024)S(1)} %add.330), channel_id=1, source_target_pairs={{0,8},{1,9},{2,10},{3,11},{4,12},{5,13},{6,14},{7,15},{8,0},{9,1},... | collective-permute-start | bytes 12296 | tf_op jit(solution)/shard_map/ppermute | solution.py:984
  310.1 18.2 %collective-permute-start.30 = (bf16[192,1024]{1,0:T(8,128)(2,1)}, bf16[192,1024]{1,0:T(8,128)(2,1)S(1)}, u32[]{:S(2)}, u32[]{:S(2)}) collective-permute-start(bf16[192,1024]{1,0:T(8,128)(2,1)} %pad_maximum_fusion.10), channel_id=1, source_target_pairs={{0,1},{1,0},{2,3},{3,2},{4,5},{5,4},{6,7},{7,6},{8,9},{9,8},{10,11... | collective-permute-start | bytes 1179656 | tf_op jit(solution)/shard_map/ppermute | solution.py:902
  312.0 23.9 %collective-permute-start.36 = (bf16[192,1024]{1,0:T(8,128)(2,1)}, bf16[192,1024]{1,0:T(8,128)(2,1)S(1)}, u32[]{:S(2)}, u32[]{:S(2)}) collective-permute-start(bf16[192,1024]{1,0:T(8,128)(2,1)} %pad_maximum_fusion.11), channel_id=1, source_target_pairs={{0,1},{1,0},{2,3},{3,2},{4,5},{5,4},{6,7},{7,6},{8,9},{9,8},{10,11... | collective-permute-start | bytes 1179656 | tf_op jit(solution)/shard_map/ppermute | solution.py:902
  323.8 21.7 %collective-permute-start.8 = (f32[1024]{0:T(1024)S(1)}, f32[1024]{0:T(1024)S(1)}, u32[]{:S(2)}, u32[]{:S(2)}) collective-permute-start(f32[1024]{0:T(1024)S(1)} %add.331), channel_id=1, source_target_pairs={{0,16},{1,17},{2,18},{3,19},{4,20},{5,21},{6,22},{7,23},{8,24},{9,... | collective-permute-start | bytes 12296 | tf_op jit(solution)/shard_map/ppermute | solution.py:984
  327.1 22.5 %collective-permute-start.16 = (bf16[192,1024]{1,0:T(8,128)(2,1)}, bf16[192,1024]{1,0:T(8,128)(2,1)S(1)}, u32[]{:S(2)}, u32[]{:S(2)}) collective-permute-start(bf16[192,1024]{1,0:T(8,128)(2,1)} %pad_maximum_fusion.9), channel_id=1, source_target_pairs={{0,1},{1,0},{2,3},{3,2},{4,5},{5,4},{6,7},{7,6},{8,9},{9,8},{10,11... | collective-permute-start | bytes 1179656 | tf_op jit(solution)/shard_map/ppermute | solution.py:902
  330.6 22.4 %collective-permute-start.31 = (bf16[384,1024]{1,0:T(8,128)(2,1)}, bf16[384,1024]{1,0:T(8,128)(2,1)}, u32[]{:S(2)}, u32[]{:S(2)}) collective-permute-start(bf16[384,1024]{1,0:T(8,128)(2,1)} %pad_maximum_fusion.4), channel_id=1, source_target_pairs={{0,8},{1,9},{2,10},{3,11},{4,12},{5,13},{6,14},{7,15},{8,0},{9,1},... | collective-permute-start | bytes 2359304 | tf_op jit(solution)/shard_map/ppermute | solution.py:902
  337.0 18.1 %collective-permute-start.37 = (bf16[384,1024]{1,0:T(8,128)(2,1)}, bf16[384,1024]{1,0:T(8,128)(2,1)}, u32[]{:S(2)}, u32[]{:S(2)}) collective-permute-start(bf16[384,1024]{1,0:T(8,128)(2,1)} %pad_maximum_fusion.5), channel_id=1, source_target_pairs={{0,8},{1,9},{2,10},{3,11},{4,12},{5,13},{6,14},{7,15},{8,0},{9,1},... | collective-permute-start | bytes 2359304 | tf_op jit(solution)/shard_map/ppermute | solution.py:902
  343.4 73.4 %collective-permute-start.1 = (bf16[176,1024]{1,0:T(8,128)(2,1)S(1)}, bf16[176,1024]{1,0:T(8,128)(2,1)}, u32[]{:S(2)}, u32[]{:S(2)}) collective-permute-start(bf16[176,1024]{1,0:T(8,128)(2,1)S(1)} %copy-done.11), channel_id=1, source_target_pairs={{0,0},{1,1},{2,16},{3,17},{4,8},{5,9},{6,24},{7,25},{8,2},{9,3},{1... | collective-permute-start | bytes 1081352 | tf_op jit(solution)/shard_map/ppermute | solution.py:902
  350.7 34.0 %collective-permute-start.17 = (bf16[384,1024]{1,0:T(8,128)(2,1)S(1)}, bf16[384,1024]{1,0:T(8,128)(2,1)}, u32[]{:S(2)}, u32[]{:S(2)}) collective-permute-start(bf16[384,1024]{1,0:T(8,128)(2,1)S(1)} %pad_maximum_fusion.3), channel_id=1, source_target_pairs={{0,8},{1,9},{2,10},{3,11},{4,12},{5,13},{6,14},{7,15},{8,0},{9,1},... | collective-permute-start | bytes 2359304 | tf_op jit(solution)/shard_map/ppermute | solution.py:902
  366.7 13.7 %collective-permute-start.41 = (bf16[2,128,1024]{2,1,0:T(8,128)(2,1)S(1)}, bf16[2,128,1024]{2,1,0:T(8,128)(2,1)}, u32[]{:S(2)}, u32[]{:S(2)}) collective-permute-start(bf16[2,128,1024]{2,1,0:T(8,128)(2,1)S(1)} %dynamic-slice_bitcast_fusion), channel_id=1, source_target_pairs={{0,2},{1,3},{2,0},{3,1},{4,6},{5,7},{6,4},{7,5},{8,10},{9,11},{10,... | collective-permute-start | bytes 1572872 | tf_op jit(solution)/shard_map/ppermute | solution.py:902
  377.1 20.1 %collective-permute-start.38 = (bf16[2,256,512]{2,1,0:T(8,128)(2,1)}, bf16[2,256,512]{2,1,0:T(8,128)(2,1)S(1)}, u32[]{:S(2)}, u32[]{:S(2)}) collective-permute-start(bf16[2,256,512]{2,1,0:T(8,128)(2,1)} %dynamic-slice_bitcast_fusion.1), channel_id=1, source_target_pairs={{0,2},{1,3},{2,0},{3,1},{4,6},{5,7},{6,4},{7,5},{8,10},{9,11},{10,... | collective-permute-start | bytes 1572872 | tf_op jit(solution)/shard_map/ppermute | solution.py:902
  381.9 13.5 %collective-permute-start.42 = (bf16[128,1024]{1,0:T(8,128)(2,1)S(1)}, bf16[128,1024]{1,0:T(8,128)(2,1)S(1)}, u32[]{:S(2)}, u32[]{:S(2)}) collective-permute-start(bf16[128,1024]{1,0:T(8,128)(2,1)S(1)} %dynamic-slice_bitcast_fusion.3), channel_id=1, source_target_pairs={{0,4},{1,5},{2,6},{3,7},{4,0},{5,1},{6,2},{7,3},{8,12},{9,13},{10,... | collective-permute-start | bytes 786440 | tf_op jit(solution)/shard_map/ppermute | solution.py:902
  396.2 44.2 %all-gather.6.cloned.1.call-start = ((), (), s32[]{:S(2)}) async-start(), calls=%async_computation.4 | async-start | bytes 1310720 | tf_op jit(solution)/shard_map/all_gather | solution.py:976
  398.4 13.7 %collective-permute-start.39 = (bf16[256,512]{1,0:T(8,128)(2,1)S(1)}, bf16[256,512]{1,0:T(8,128)(2,1)S(1)}, u32[]{:S(2)}, u32[]{:S(2)}) collective-permute-start(bf16[256,512]{1,0:T(8,128)(2,1)S(1)} %dynamic-slice_bitcast_fusion.4), channel_id=1, source_target_pairs={{0,4},{1,5},{2,6},{3,7},{4,0},{5,1},{6,2},{7,3},{8,12},{9,13},{10,... | collective-permute-start | bytes 786440 | tf_op jit(solution)/shard_map/ppermute | solution.py:902
  403.5 10.0 %collective-permute-start.18 = (bf16[2,256,128]{2,1,0:T(8,128)(2,1)S(1)}, bf16[2,256,128]{2,1,0:T(8,128)(2,1)S(1)}, u32[]{:S(2)}, u32[]{:S(2)}) collective-permute-start(bf16[2,256,128]{2,1,0:T(8,128)(2,1)S(1)} %dynamic-slice_bitcast_fusion.9), channel_id=1, source_target_pairs={{0,2},{1,3},{2,0},{3,1},{4,6},{5,7},{6,4},{7,5},{8,10},{9,11},{10,... | collective-permute-start | bytes 393224 | tf_op jit(solution)/shard_map/ppermute | solution.py:902
  412.2 3.9 collective-permute-start.40
  413.5 7.3 %collective-permute-start.19 = (bf16[256,128]{1,0:T(8,128)(2,1)S(1)}, bf16[256,128]{1,0:T(8,128)(2,1)S(1)}, u32[]{:S(2)}, u32[]{:S(2)}) collective-permute-start(bf16[256,128]{1,0:T(8,128)(2,1)S(1)} %dynamic-slice_bitcast_fusion.13), channel_id=1, source_target_pairs={{0,4},{1,5},{2,6},{3,7},{4,0},{5,1},{6,2},{7,3},{8,12},{9,13},{10,... | collective-permute-start | bytes 196616 | tf_op jit(solution)/shard_map/ppermute | solution.py:902
  420.9 2.8 collective-permute-start.20
  426.6 15.4 %collective-permute-start.2 = (bf16[2,64,1024]{2,1,0:T(8,128)(2,1)S(1)}, bf16[2,64,1024]{2,1,0:T(8,128)(2,1)S(1)}, u32[]{:S(2)}, u32[]{:S(2)}) collective-permute-start(bf16[2,64,1024]{2,1,0:T(8,128)(2,1)S(1)} %dynamic-slice_bitcast_fusion.5), channel_id=1, source_target_pairs={{0,2},{1,3},{2,0},{3,1},{4,6},{5,7},{6,4},{7,5},{8,10},{9,11},{10,... | collective-permute-start | bytes 786440 | tf_op jit(solution)/shard_map/ppermute | solution.py:902
  442.7 9.0 %collective-permute-start.3 = (bf16[64,1024]{1,0:T(8,128)(2,1)}, bf16[64,1024]{1,0:T(8,128)(2,1)S(1)}, u32[]{:S(2)}, u32[]{:S(2)}) collective-permute-start(bf16[64,1024]{1,0:T(8,128)(2,1)} %dynamic-slice_bitcast_fusion.10), channel_id=1, source_target_pairs={{0,4},{1,5},{2,6},{3,7},{4,0},{5,1},{6,2},{7,3},{8,12},{9,13},{10,... | collective-permute-start | bytes 393224 | tf_op jit(solution)/shard_map/ppermute | solution.py:902
  (42 other events, 449.7 us)
Sparse Core Ops, SparseCore 0:
  300.9 47.0 all-gather.3
  396.3 18.0 all-gather.7
  417.0 18.8 all-gather.5
where the time goes:
time: 479 us; the launch traced here: 469 us
  local copies, waits for them, and re-layouts  110 us (23%)
  Pallas kernels  91.9 us (19%)
  starting transfers between devices  62.6 us (13%)
  matrix products  58.4 us (12%)
  waiting for transfers between devices  55.2 us (12%)
  other arithmetic  47 us (10%)
  blocking collectives  29.1 us (6%)
  between operations  14.9 us (3%)
    pallas_call x1, Pallas kernels, call_first(): pl.pallas_call(first_kernel, in_specs=[vmem] + [any_space] * 5 + [vmem],...  76.3 us
    unnamed x117, local copies, waits for them, and re-layouts  54.5 us
    ppermute x33, waiting for transfers between devices, permute(): return lax.ppermute(v, AXES, pairs)  40.1 us
    ppermute x33, starting transfers between devices, permute(): return lax.ppermute(v, AXES, pairs)  28.8 us
    all_gather x2, blocking collectives, finish_columns(): every = lax.all_gather(both, 'u', axis=0)  21.1 us
    dot_general x5, matrix products, dot_tn(): lax.dot_general(a, b, (((0,), (0,)), ((), ())), preferred_element_type=F32)  20.8 us
    dot_general x5, matrix products, dot_nt(): lax.dot_general(a, b, (((1,), (1,)), ((), ())), preferred_element_type=F32)  20.3 us
    concatenate x12, other arithmetic, gather_plane(): piece = jnp.concatenate([piece, swap_plane(piece, bit)], axis=0)  17.5 us
  transfers between devices with their start and end apart: 49, of which 15 were waited for; matrix products, arithmetic and copies ran while one was open for 40% of the time, Pallas kernels for 3%

commit v1 on v0

--- a/solution.py
+++ b/solution.py
@@ -453,6 +453,7 @@
         end = end + lens_r[s : s + 1, 0:1]
         segment_row = segment_row + jnp.where(at >= end, 1.0, 0.0)
 
+    lse[2:3, :] = segment_row
     for copy in sent_entry:
         copy.wait_recv()
     entry = ent_r[...].astype(F32)
@@ -584,6 +585,678 @@
     )(lens, inputs, skip_in, cotangent, w_skip, w_qkv, gain_one)
 
 
+def rms_back_rows(hidden, inverse, gain, grad):
+    scaled = hidden * inverse
+    weighted = grad * gain
+    inner = jnp.mean(weighted * scaled, axis=-1, keepdims=True)
+    return inverse * (weighted - scaled * inner), jnp.sum(grad * scaled, axis=0, keepdims=True)
+
+
+class PlaneGather:
+    LOW, HIGH = 80, 96
+
+    def __init__(self, sender, buffer, peers):
+        self.sender, self.buffer, self.peers = sender, buffer, peers
+
+    def block(self, k, start=0, size=TOK):
+        return self.buffer.at[rows_of(self.peers[k][1], start, size)]
+
+    def pass_on(self, k, to, start=0, size=TOK):
+        block = self.block(k, start, size)
+        copy = self.sender.remote(block, block, self.peers[to][0])
+        copy.start()
+        self.copies.append(copy)
+        return copy
+
+    def start(self):
+        self.copies = []
+        self.x = self.pass_on(0, 1)
+        self.y = self.pass_on(0, 4)
+        self.waits = [self.pass_on(0, 2)]
+
+    def forward(self):
+        self.x.wait_recv()
+        self.over_y = self.pass_on(1, 4, self.LOW, self.HIGH)
+        self.waits.append(self.pass_on(1, 2))
+        self.y.wait_recv()
+        self.over_x = self.pass_on(4, 1, 0, self.LOW)
+        self.waits.append(self.pass_on(4, 2))
+
+    def corner(self):
+        self.over_x.wait_recv()
+        self.over_y.wait_recv()
+        self.waits.append(self.pass_on(5, 2))
+
+    def done(self):
+        for copy in self.waits:
+            copy.wait_recv()
+        for copy in self.copies:
+            copy.wait_send()
+
+
+class PlaneSum:
+    def __init__(self, sender, terms, first, second, third, place):
+        self.sender, self.terms = sender, terms
+        self.first, self.second, self.third = first, second, third
+        u, z, x = place
+        self.low, self.high = lax.rem(z, 2), lax.div(z, 2)
+        self.near, self.far = (u, flip_low(z), x), (u, flip_high(z), x)
+        self.rows = third.shape[0]
+
+    def chunk(self, j, low):
+        return pl.ds(pl.multiple_of((2 * j + low) * self.rows, self.rows), self.rows)
+
+    def start(self):
+        self.waits = [
+            self.sender.push(
+                self.terms.at[self.chunk(j, 1 - self.low)], self.first.at[j], self.near
+            )
+            for j in range(2)
+        ]
+
+    def middle(self):
+        for copy in self.waits:
+            copy.wait_recv()
+        for j in range(2):
+            own = self.terms[self.chunk(j, self.low), :].astype(F32)
+            self.second[j] = (own + self.first[j].astype(F32)).astype(BF)
+        self.wait = self.sender.push(self.second.at[1 - self.high], self.third, self.far)
+
+    def end(self, out):
+        self.wait.wait_recv()
+        out[...] = (self.second[self.high].astype(F32) + self.third[...].astype(F32)).astype(BF)
+
+
+def second_kernel(
+    entry_ref,
+    cot_ref,
+    joined_ref,
+    normed_ref,
+    q_ref,
+    k_ref,
+    v_ref,
+    o_ref,
+    lse_ref,
+    cos_ref,
+    sin_ref,
+    seg_ref,
+    mixed_ref,
+    w_out_ref,
+    w_up_ref,
+    w_down_ref,
+    w_qkv_ref,
+    w_skip_ref,
+    gain_one_ref,
+    gain_two_ref,
+    b_up_ref,
+    b_up_own_ref,
+    b_down_ref,
+    result_out,
+    inputs_out,
+    skip_out,
+    g_skip_out,
+    g_qkv_out,
+    g_out_out,
+    g_up_out,
+    g_down_out,
+    vector_out,
+    wide_a,
+    wide_b,
+    w_out,
+    n2,
+    ct,
+    db,
+    joined,
+    q,
+    k,
+    v,
+    o,
+    grad,
+    lse,
+    cos_t,
+    sin_t,
+    seg,
+    entry,
+    mixed,
+    middle,
+    down_sum,
+    normed_sum,
+    result,
+    result_r,
+    d_mixed,
+    d_heads,
+    d_frames,
+    entry_r,
+    gd,
+    gu,
+    gq,
+    gs,
+    go,
+    d1,
+    d2,
+    d3,
+    dz,
+    u1,
+    u2,
+    u3,
+    uz,
+    q1,
+    q2,
+    q3,
+    qz,
+    s1,
+    s2,
+    s3,
+    sz,
+    o1,
+    o2,
+    fin_d,
+    fin_u,
+    fin_q,
+    fin_s,
+    fin_o,
+    vec,
+    vec_plane,
+    vec_sum,
+    vec_z,
+    acc,
+    send,
+    recv,
+    load,
+    spread,
+):
+    u, z, x = (lax.axis_index(a) for a in AXES)
+    me = 2 * u + x
+    peers = plane_peers(u, z, x)
+    place = (u, z, x)
+    d = entry.shape[1]
+    group = n2.shape[0]
+    hidden = wide_a.shape[1]
+    own_home = swap_bits(z)
+    home = (own_home, u, x)
+    stays = jnp.logical_and(own_home == u, u == z)
+    sender = Sender(send, recv, load)
+    mine = rows_of(me)
+
+    got_cot = sender.local(cot_ref, ct.at[mine])
+    got_entry = sender.local(entry_ref, entry)
+    got_mixed = sender.local(mixed_ref, mixed)
+    got_out = sender.local(w_out_ref, w_out)
+    got_up = sender.local(w_up_ref, wide_a)
+    got_down = sender.local(w_down_ref, wide_b)
+    got_heads = [
+        sender.local(a, b)
+        for a, b in (
+            (q_ref, q),
+            (k_ref, k),
+            (v_ref, v),
+            (o_ref, o),
+            (lse_ref, lse),
+            (cos_ref, cos_t),
+            (sin_ref, sin_t),
+            (seg_ref, seg),
+            (joined_ref, joined),
+        )
+    ]
+    got_cot.wait()
+    gather_cot = PlaneGather(sender, ct, peers)
+    gather_cot.start()
+
+    got_entry.wait()
+    got_mixed.wait()
+    got_out.wait()
+    value = entry[...].astype(F32) + dot_nn(mixed[...], w_out[...])
+    middle[...] = value
+    n2[mine, :] = (value * rms_parts(value) * gain_two_ref[...]).astype(BF)
+    gather_normed = PlaneGather(sender, n2, peers)
+    gather_normed.start()
+
+    down_sum[...] = jnp.zeros_like(down_sum)
+    normed_sum[...] = jnp.zeros_like(normed_sum)
+    got_up.wait()
+    got_down.wait()
+    step = 512
+
+    def feed(c, _):
+        cols = pl.ds(pl.multiple_of(c * step, step), step)
+        up = dot_nn(n2[mine, :], wide_a[:, cols]) + b_up_ref[pl.ds(c, 1), :]
+        active, slope = gelu_both(up)
+        d_up = (dot_nt(ct[mine, :], wide_b[cols, :]) * slope).astype(BF)
+        down_sum[...] += dot_nn(active.astype(BF), wide_b[cols, :])
+        normed_sum[...] += dot_nt(d_up, wide_a[:, cols])
+        vec[pl.ds(8 + c, 1), :] = jnp.sum(d_up.astype(F32), axis=0, keepdims=True)
+        return 0
+
+    half = hidden // step // 2
+    lax.fori_loop(0, half, feed, 0)
+    gather_cot.forward()
+    lax.fori_loop(half, 2 * half, feed, 0)
+    gather_cot.corner()
+
+    value = middle[...]
+    result[...] = (value + down_sum[...] + b_down_ref[...]).astype(BF)
+    sent_result = sender.push_or_keep(result, result_r, home, stays)
+    inverse = rms_parts(value)
+    back, g_gain_two = rms_back_rows(value, inverse, gain_two_ref[...], normed_sum[...])
+    grad_out = ct[mine, :].astype(F32)
+    d_middle = grad_out + back
+    middle[...] = d_middle
+    g_b_down = jnp.sum(grad_out, axis=0, keepdims=True)
+    for i in range(2):
+        part = slice(i * d // 2, (i + 1) * d // 2)
+        vec[2 + i : 3 + i, :] = g_gain_two[:, part]
+        vec[4 + i : 5 + i, :] = g_b_down[:, part]
+    vec[6:8, :] = jnp.zeros((2, step), F32)
+    db[mine, :] = d_middle.astype(BF)
+    d_mixed[...] = dot_nt(db[mine, :], w_out[...]).astype(BF)
+    own_grad = sender.local(
+        d_mixed.at[:, pl.ds(pl.multiple_of(me * 128, 128), 128)], grad.at[mine]
+    )
+    got_grad = [
+        sender.push(
+            d_mixed.at[:, pl.ds(pl.multiple_of(peers[i][1] * 128, 128), 128)],
+            grad.at[mine],
+            peers[i][0],
+        )
+        for i in range(1, 8)
+    ]
+    gather_normed.forward()
+    gather_branch = PlaneGather(sender, db, peers)
+    gather_branch.start()
+    gather_normed.corner()
+    gather_cot.done()
+    gather_normed.done()
+
+    chunk = hidden // 32
+
+    def own_units(w_up_own, w_down_own, active, d_up):
+        copies = []
+        for s in range(4):
+            first = pl.multiple_of((2 * s + x) * (4 * chunk) + u * chunk, chunk)
+            copies.append(
+                sender.local(w_up_ref.at[:, pl.ds(first, chunk)], w_up_own.at[:, pl.ds(s * chunk, chunk)])
+            )
+            copies.append(
+                sender.local(w_down_ref.at[pl.ds(first, chunk)], w_down_own.at[pl.ds(s * chunk, chunk)])
+            )
+        for copy in copies:
+            copy.wait()
+
+        def units(i, _):
+            rows = rows_of(i)
+            up = dot_nn(n2[rows, :], w_up_own[...]) + b_up_own_ref[...]
+            act, slope = gelu_both(up)
+            active[rows, :] = act.astype(BF)
+            d_up[rows, :] = (dot_nt(ct[rows, :], w_down_own[...]) * slope).astype(BF)
+            return 0
+
+        lax.fori_loop(0, group // TOK, units, 0)
+
+        def down_terms(i, _):
+            cols = pl.ds(pl.multiple_of(i * 256, 256), 256)
+            gd[cols, :] = dot_tn(active[:, cols], ct[...]).astype(BF)
+            return 0
+
+        lax.fori_loop(0, 4 * chunk // 256, down_terms, 0)
+
+        def up_terms(i, _):
+            cols = pl.ds(pl.multiple_of(i * 256, 256), 256)
+            gu[cols, :] = dot_tn(n2[:, cols], d_up[...]).astype(BF)
+            return 0
+
+        lax.fori_loop(0, d // 256, up_terms, 0)
+
+    pl.run_scoped(
+        own_units,
+        pltpu.VMEM((d, 4 * chunk), BF),
+        pltpu.VMEM((4 * chunk, d), BF),
+        pltpu.VMEM((group, 4 * chunk), BF),
+        pltpu.VMEM((group, 4 * chunk), BF),
+    )
+    sum_down = PlaneSum(sender, gd, d1, d2, d3, place)
+    sum_up = PlaneSum(sender, gu, u1, u2, u3, place)
+    sum_down.start()
+    sum_up.start()
+    gather_branch.forward()
+    got_normed = sender.local(normed_ref, ct)
+    got_qkv = sender.local(w_qkv_ref, wide_a.at[:, pl.ds(0, 3 * d)])
+    got_skip = sender.local(w_skip_ref, wide_b.at[pl.ds(0, 2 * d)])
+    for copy in got_heads:
+        copy.wait()
+    own_grad.wait()
+    for copy in got_grad:
+        copy.wait_recv()
+
+    def heads(dq, dk, dv):
+        backward_heads(
+            q, k, v, o, grad, seg, lse[2:3, :], lse, dq, dk, dv, acc
+        )
+
+        def turn_back(i, _):
+            rows = rows_of(i)
+            cosine, sine = cos_t[rows, :], sin_t[rows, :]
+            front = lax.rem(lax.broadcasted_iota(jnp.int32, (TOK, 128), 1), 64) < 32
+            for c, ref in ((0, dq), (1, dk)):
+                t = ref[rows, :].astype(BF).astype(F32)
+                swapped = jnp.where(front, pltpu.roll(t, 96, 1), pltpu.roll(t, 32, 1))
+                d_heads[c, rows, :] = (t * cosine - swapped * sine).astype(BF)
+            d_heads[2, rows, :] = dv[rows, :].astype(BF)
+            return 0
+
+        lax.fori_loop(0, group // TOK, turn_back, 0)
+
+    pl.run_scoped(heads, *[pltpu.VMEM((group, 128), F32)] * 3)
+    own_frames = sender.local(
+        d_heads.at[:, mine], d_frames.at[:, :, pl.ds(pl.multiple_of(me * 128, 128), 128)]
+    )
+    got_frames = [
+        sender.push(
+            d_heads.at[:, rows_of(peers[i][1])],
+            d_frames.at[:, :, pl.ds(pl.multiple_of(me * 128, 128), 128)],
+            peers[i][0],
+        )
+        for i in range(1, 8)
+    ]
+    gather_branch.corner()
+    sum_down.middle()
+    sum_up.middle()
+    got_normed.wait()
+
+    def qkv_terms(i, _):
+        cols = pl.ds(pl.multiple_of(i * 256, 256), 256)
+        turned = ct[:, cols].T
+        for c in range(3):
+            gq[cols, c * 128 : (c + 1) * 128] = dot_nn(turned, d_heads[c]).astype(BF)
+        return 0
+
+    lax.fori_loop(0, d // 256, qkv_terms, 0)
+    sum_qkv = PlaneSum(sender, gq, q1, q2, q3, place)
+    sum_qkv.start()
+    gather_branch.done()
+    go[...] = dot_tn(o[...], db[...]).astype(BF)
+
+    same_high = lax.div(z, 2) == lax.div(u, 2)
+    same_low = lax.rem(z, 2) == lax.rem(u, 2)
+    owner = z == u
+    to_far = sender.remote(go, o1, (u, flip_high(z), x))
+    to_near = sender.remote(go, o2, (u, flip_low(z), x))
+
+    @pl.when(jnp.logical_not(same_high))
+    def _():
+        to_far.start()
+
+    own_frames.wait()
+    for copy in got_frames:
+        copy.wait_recv()
+    got_qkv.wait()
+    d_normed = dot_nt(d_frames[0], wide_a[:, :d])
+    d_normed += dot_nt(d_frames[1], wide_a[:, d : 2 * d])
+    d_normed += dot_nt(d_frames[2], wide_a[:, 2 * d : 3 * d])
+    value = entry[...].astype(F32)
+    back, g_gain_one = rms_back_rows(value, rms_parts(value), gain_one_ref[...], d_normed)
+    for i in range(2):
+        vec[i : i + 1, :] = g_gain_one[:, i * d // 2 : (i + 1) * d // 2]
+    n2[mine, :] = (middle[...] + back).astype(BF)
+    gather_entry = PlaneGather(sender, n2, peers)
+    gather_entry.start()
+    sent_entry = sender.push_or_keep(n2.at[mine], entry_r, home, stays)
+
+    got_vec = [
+        sender.push(vec, vec_plane.at[pl.ds(pl.multiple_of(me * 16, 16), 16)], peers[i][0])
+        for i in range(1, 8)
+    ]
+    vec_plane[pl.ds(pl.multiple_of(me * 16, 16), 16), :] = vec[...]
+
+    @pl.when(same_high)
+    def _():
+        to_far.wait_recv()
+        go[...] = (go[...].astype(F32) + o1[...].astype(F32)).astype(BF)
+
+    sum_qkv.middle()
+    sum_down.end(dz)
+    sum_up.end(uz)
+
+    final_d = [
+        sender.push(dz, fin_d.at[pl.ds(pl.multiple_of(u * 128, 128), 128)], peers[i][0])
+        for i in (2, 4, 6)
+    ]
+    fin_d[pl.ds(pl.multiple_of(u * 128, 128), 128), :] = dz[...]
+
+    def rows_for(device, rows):
+        return pl.ds(pl.multiple_of(device[2] * rows, rows), rows)
+
+    def to_columns(source, fin):
+        copies = [
+            sender.push(source.at[rows_for(peers[i][0], 128)], fin.at[me], peers[i][0])
+            for i in range(1, 8)
+        ]
+        fin[me] = source[rows_for(place, 128), :]
+        return copies
+
+    final_u = to_columns(uz, fin_u)
+
+    @pl.when(jnp.logical_and(same_high, jnp.logical_not(same_low)))
+    def _():
+        to_near.start()
+
+    @pl.when(owner)
+    def _():
+        to_near.wait_recv()
+        fin_o[...] = (go[...].astype(F32) + o2[...].astype(F32)).astype(BF)
+
+    tell = [
+        pltpu.make_async_remote_copy(
+            src_ref=fin_o,
+            dst_ref=fin_o,
+            send_sem=spread.at[i],
+            recv_sem=spread.at[3],
+            device_id=peers[2 * (i + 1)][0],
+            device_id_type=MESH_ID,
+        )
+        for i in range(3)
+    ]
+
+    @pl.when(owner)
+    def _():
+        for copy in tell:
+            copy.start()
+
+    def skip_terms(i):
+        rows = rows_of(peers[i][1])
+        return dot_tn(joined[rows, :], n2[rows, :])
+
+    total = skip_terms(0)
+    gather_entry.forward()
+    total += skip_terms(1)
+    total += skip_terms(4)
+    gather_entry.corner()
+    total += skip_terms(5)
+    gather_entry.done()
+    for i in (2, 3, 6, 7):
+        total += skip_terms(i)
+    gs[...] = total.astype(BF)
+    sum_skip = PlaneSum(sender, gs, s1, s2, s3, place)
+    sum_skip.start()
+
+    for copy in got_vec:
+        copy.wait_recv()
+    value = vec_plane[0:16, :]
+    for i in range(1, 8):
+        value += vec_plane[16 * i : 16 * (i + 1), :]
+    vec_sum[...] = value
+    z_devices = (
+        (u, flip_low(z), x),
+        (u, flip_high(z), x),
+        (u, flip_low(flip_high(z)), x),
+    )
+    got_vec = [
+        sender.push(vec_sum, vec_z.at[pl.ds(pl.multiple_of(z * 16, 16), 16)], device)
+        for device in z_devices
+    ]
+    vec_z[pl.ds(pl.multiple_of(z * 16, 16), 16), :] = vec_sum[...]
+
+    sum_qkv.end(qz)
+    final_q = to_columns(qz, fin_q)
+
+    sent_entry.wait_recv()
+    got_skip.wait()
+    outs = []
+    for i, (staged, out) in enumerate(((mixed, inputs_out), (entry, skip_out))):
+        staged[...] = dot_nt(entry_r[...], wide_b[i * d : (i + 1) * d, :]).astype(BF)
+        outs.append(sender.local(staged, out))
+    sum_skip.middle()
+    for copy in got_vec:
+        copy.wait_recv()
+    vec_sum_out = vec_z[0:16, :] + vec_z[16:32, :] + vec_z[32:48, :] + vec_z[48:64, :]
+    vec_plane[0:16, :] = vec_sum_out
+    outs.append(sender.local(vec_plane.at[pl.ds(0, 16)], vector_out))
+    sent_result.wait_recv()
+    outs.append(sender.local(result_r, result_out))
+    for copy in final_d + final_u + final_q:
+        copy.wait_recv()
+    outs.append(sender.local(fin_d, g_down_out))
+    for p in range(8):
+        for s in range(4):
+            first = (2 * s + p % 2) * 4 * chunk + p // 2 * chunk
+            outs.append(
+                sender.local(
+                    fin_u.at[p, :, pl.ds(s * chunk, chunk)], g_up_out.at[:, pl.ds(first, chunk)]
+                )
+            )
+        for c in range(3):
+            outs.append(
+                sender.local(
+                    fin_q.at[p, :, pl.ds(c * 128, 128)],
+                    g_qkv_out.at[:, pl.ds(c * d + p * 128, 128)],
+                )
+            )
+
+    @pl.when(owner)
+    def _():
+        for copy in tell:
+            copy.wait_send()
+
+    @pl.when(jnp.logical_not(same_high))
+    def _():
+        to_far.wait_send()
+
+    @pl.when(jnp.logical_and(same_high, jnp.logical_not(same_low)))
+    def _():
+        to_near.wait_send()
+
+    @pl.when(jnp.logical_not(owner))
+    def _():
+        tell[0].wait_recv()
+
+    outs.append(sender.local(fin_o, g_out_out))
+    sum_skip.end(sz)
+    final_s = [
+        sender.push(sz, fin_s.at[pl.ds(pl.multiple_of(u * 64, 64), 64)], peers[i][0])
+        for i in (2, 4, 6)
+    ]
+    fin_s[pl.ds(pl.multiple_of(u * 64, 64), 64), :] = sz[...]
+    for copy in final_s:
+        copy.wait_recv()
+    outs.append(sender.local(fin_s, g_skip_out))
+    for copy in outs:
+        copy.wait()
+    sender.finish()
+
+
+def call_second(own, weights, vectors):
+    d = weights[0].shape[0]
+    group = 8 * TOK
+    hidden = weights[1].shape[1]
+    any_space = pl.BlockSpec(memory_space=pl.ANY)
+    vmem = pl.BlockSpec(memory_space=pltpu.VMEM)
+    block, wide = ((TOK, d), BF), ((group, d), BF)
+    head, table, total = ((group, 128), BF), ((group, 128), F32), ((TOK, d), F32)
+    unit = hidden // 8
+
+    def sums(rows, columns):
+        return [
+            ((2, rows, columns), BF),
+            ((2, rows, columns), BF),
+            ((rows, columns), BF),
+            ((rows, columns), BF),
+        ]
+
+    outs = [
+        block,
+        block,
+        block,
+        ((2 * d // 8, d), BF),
+        ((d // 8, 3 * d), BF),
+        ((d // 8, d), BF),
+        ((d // 8, hidden), BF),
+        ((unit, d), BF),
+        ((16, 512), F32),
+    ]
+    scratch = [
+        ((d, hidden), BF),
+        ((hidden, d), BF),
+        ((d, d), BF),
+        wide,
+        wide,
+        wide,
+        ((group, 256), BF),
+        head,
+        head,
+        head,
+        head,
+        head,
+        ((8, group), F32),
+        table,
+        table,
+        table,
+        block,
+        block,
+        total,
+        total,
+        total,
+        block,
+        block,
+        block,
+        ((3, group, 128), BF),
+        ((3, TOK, d), BF),
+        block,
+        ((unit, d), BF),
+        ((d, unit), BF),
+        ((d, 384), BF),
+        ((256, d), BF),
+        ((128, d), BF),
+        *sums(unit // 4, d),
+        *sums(d // 4, unit),
+        *sums(d // 4, 384),
+        *sums(64, d),
+        ((128, d), BF),
+        ((128, d), BF),
+        ((unit, d), BF),
+        ((8, d // 8, unit), BF),
+        ((8, d // 8, 384), BF),
+        ((256, d), BF),
+        ((128, d), BF),
+        ((16, 512), F32),
+        ((128, 512), F32),
+        ((16, 512), F32),
+        ((64, 512), F32),
+        ((128, group), F32),
+    ]
+    return pl.pallas_call(
+        second_kernel,
+        in_specs=[any_space] * (len(own) + len(weights)) + [vmem] * len(vectors),
+        out_specs=[any_space] * len(outs),
+        out_shape=[jax.ShapeDtypeStruct(*o) for o in outs],
+        scratch_shapes=[pltpu.VMEM(*s) for s in scratch]
+        + [pltpu.SemaphoreType.DMA((128,))] * 2
+        + [pltpu.SemaphoreType.DMA((128,)), pltpu.SemaphoreType.DMA((4,))],
+        compiler_params=pltpu.CompilerParams(
+            vmem_limit_bytes=60 * 2**20, has_side_effects=True
+        ),
+        name="mixed_to_gradients",
+    )(*own, *weights, *vectors)
+
+
 def local(
     sizes,
     inputs,
@@ -881,263 +1554,41 @@
     b_down,
 ):
     n_u, n_z, n_x = sizes
-    frames, d = inputs.shape
+    d = inputs.shape[1]
     hidden = w_up.shape[1]
-    parts = n_u * n_x
-    group = frames * parts
-    u, z, x = (lax.axis_index(a) for a in AXES)
-    me = u * n_x + x
-    width = d // parts
-
-    def line(a, b, c):
-        return (a * n_z + b) * n_x + c
-
-    def permute(v, to):
-        pairs = [
-            (line(a, b, c), line(*to(a, b, c)))
-            for a in range(n_u)
-            for b in range(n_z)
-            for c in range(n_x)
-        ]
-        return lax.ppermute(v, AXES, pairs)
-
-    def plane_of(a):
-        return (a % 2) * (n_u // 2) + a // 2
-
-    group_of = {plane_of(a): a for a in range(n_u)}
-
-    def away(v):
-        return permute(v, lambda a, b, c: (b, plane_of(a), c))
-
-    def home(v):
-        return permute(v, lambda a, b, c: (group_of[b], a, c))
-
-    def swap_plane(v, bit):
-        def to(a, b, c):
-            other = (a * n_x + c) ^ bit
-            return other // n_x, b, other % n_x
-
-        return permute(v, to)
-
-    plane_bits = [1 << i for i in range(parts.bit_length() - 1)]
-    if n_x == 2 and n_u == 4:
-        orders = ([1, 4, 2], [4, 1, 2])
-    else:
-        orders = (plane_bits, plane_bits)
-    cut = frames // 32 * 16
-
-    def gather_plane(v):
-        pieces = []
-        for piece, order in zip((v[:cut], v[cut:]), orders):
-            for bit in order:
-                piece = jnp.concatenate([piece, swap_plane(piece, bit)], axis=0)
-            pieces.append(piece)
-        return jnp.concatenate(pieces, axis=0)
-
-    def gather_order(v):
-        pieces = []
-        for start, size, order in ((0, cut, orders[0]), (cut, frames - cut, orders[1])):
-            offsets = [0]
-            for bit in order:
-                offsets = offsets + [o ^ bit for o in offsets]
-            for o in offsets:
-                pieces.append(
-                    lax.dynamic_slice_in_dim(v, (me ^ o) * frames + start, size, axis=0)
-                )
-        return jnp.concatenate(pieces, axis=0)
-
-    z_bits = n_z.bit_length() - 1
-
-    def reduce_z(v):
-        rest = v.shape[1:]
-        v = v.reshape((2,) * z_bits + (v.shape[0] // n_z,) + rest)
-        for bit in range(z_bits):
-            axis = z_bits - 1 - bit
-            own = (z >> bit) & 1
-            keep = lax.dynamic_index_in_dim(v, own, axis, keepdims=False)
-            give = lax.dynamic_index_in_dim(v, 1 - own, axis, keepdims=False)
-            got = permute(
-                give.astype(BF), lambda a, b, c, bit=bit: (a, b ^ (1 << bit), c)
-            )
-            v = keep.astype(F32) + got.astype(F32)
-            if bit < z_bits - 1:
-                v = v.astype(BF)
-        return v.astype(BF)
-
-    def finish_columns(v):
-        if n_x == 2:
-            v = v.reshape((2, v.shape[0] // 2) + v.shape[1:])
-            keep = lax.dynamic_index_in_dim(v, x, 0, keepdims=False)
-            give = lax.dynamic_index_in_dim(v, 1 - x, 0, keepdims=False)
-            got = permute(give, lambda a, b, c: (a, b, 1 - c))
-            both = jnp.where(x == 0, jnp.stack([keep, got]), jnp.stack([got, keep]))
-        else:
-            both = v[None]
-        every = lax.all_gather(both, "u", axis=0)
-        return every.reshape((parts,) + both.shape[1:])
-
-    def sum_all(v):
-        total = n_u * n_z * n_x
-        for i in range(total.bit_length() - 1):
-            bit = 1 << i
-            pairs = [(n, n ^ bit) for n in range(total)]
-            v = v + lax.ppermute(v, AXES, pairs)
-        return v
-
+    u, x = lax.axis_index("u"), lax.axis_index("x")
     lens = jnp.broadcast_to(
         jnp.pad(lengths[0].astype(F32), (0, 8 - lengths.shape[1]))[:, None], (8, 128)
     )
-    (
-        entry_low,
-        grad_low,
-        joined_own,
-        plane_first,
-        head_query,
-        head_keys,
-        head_values,
-        head_mixed,
-        lse8,
-        cos_t,
-        sin_t,
-        seg_t,
-        mixed,
-    ) = call_first(lens, inputs, skip_in, cotangent, w_skip, w_qkv, gain_one[None])
-    entry = entry_low.astype(F32)
-    inverse_one = rms_parts(entry)
-    lse = lse8[:2]
-    col = seg_t[:, :1]
-    row = col.reshape(1, group)
-    own_cos = lax.dynamic_slice_in_dim(cos_t, me * frames, frames)[:, None, :64]
-    own_sin = lax.dynamic_slice_in_dim(sin_t, me * frames, frames)[:, None, :64]
-    tables = (own_cos, own_sin)
-    group_tables = (cos_t[:, None, :64], sin_t[:, None, :64])
-    def to_heads(*arrays):
-        n = len(arrays)
-        v = jnp.stack([a.reshape(frames, parts, width) for a in arrays], axis=2)
-        v = lax.all_to_all(
-            v.reshape(frames, parts * n * width), PLANE, split_axis=1, concat_axis=0, tiled=True
-        )
-        return [v[:, i * width : (i + 1) * width] for i in range(n)]
-
-    def to_frames(*arrays):
-        n = len(arrays)
-        v = jnp.concatenate(arrays, axis=1)
-        v = lax.all_to_all(v, PLANE, split_axis=0, concat_axis=1, tiled=True)
-        v = v.reshape(frames, parts, n, width)
-        return [v[:, :, i].reshape(frames, d) for i in range(n)]
-
-    middle = entry + dot_nn(mixed, w_out)
-    inverse_two = rms_parts(middle)
-    normed_two = (middle * inverse_two * gain_two).astype(BF)
-    up = dot_nn(normed_two, w_up) + b_up
-    d_active = dot_nt(grad_low, w_down)
-    active, slope = gelu_both(up)
-    d_up = (d_active * slope).astype(BF)
-    result_away = (middle + dot_nn(active.astype(BF), w_down) + b_down).astype(BF)
-    result = home(result_away)
-    d_normed_two = dot_nt(d_up, w_up)
-    middle_part, g_gain_two = rms_back(middle, inverse_two, gain_two, d_normed_two)
-    d_middle = grad_low.astype(F32) + middle_part
-    d_branch = d_middle.astype(BF)
-    d_mixed = dot_nt(d_branch, w_out).astype(BF)
-    (head_grad,) = to_heads(d_mixed)
-    dq, dk, dv = call_backward(
-        head_query, head_keys, head_values, head_mixed, head_grad, col, row, lse
-    )
-
-    chunk = hidden // (n_z * parts)
-    w_up_own = lax.dynamic_slice(
-        w_up.reshape(d, n_z, n_x, n_u, chunk), (0, 0, x, u, 0), (d, n_z, 1, 1, chunk)
-    ).reshape(d, n_z * chunk)
-    w_down_own = lax.dynamic_slice(
-        w_down.reshape(n_z, n_x, n_u, chunk, d), (0, x, u, 0, 0), (n_z, 1, 1, chunk, d)
-    ).reshape(n_z * chunk, d)
     b_up_own = lax.dynamic_slice(
-        b_up.reshape(n_z, n_x, n_u, chunk), (0, x, u, 0), (n_z, 1, 1, chunk)
-    ).reshape(n_z * chunk)
-    plane_grad = gather_plane(grad_low)
-    plane_normed = gather_plane(normed_two)
-    up_own = dot_nn(plane_normed, w_up_own) + b_up_own
-    active_own, slope_own = gelu_both(up_own)
-    d_up_own = (dot_nt(plane_grad, w_down_own) * slope_own).astype(BF)
-    g_down = dot_tn(active_own.astype(BF), plane_grad)
-    g_up = dot_tn(plane_normed, d_up_own)
-    down_z = reduce_z(g_down.astype(BF))
-    up_z = reduce_z(g_up.astype(BF))
-    out_down = lax.all_gather(down_z, "u", axis=0, tiled=True).astype(F32)
-    out_up = finish_columns(up_z)
-    out_up = (
-        out_up.reshape(n_u, n_x, -1, n_z, chunk).transpose(2, 3, 1, 0, 4).reshape(-1, hidden)
-    ).astype(F32)
-
-    plane_mixed = gather_plane(mixed)
-    own_branch = gather_order(
-        lax.all_to_all(d_branch, PLANE, split_axis=1, concat_axis=0, tiled=True)
-    )
-    g_out = dot_tn(plane_mixed, own_branch)
-    out_out = (
-        finish_columns(reduce_z(g_out.astype(BF))).transpose(1, 0, 2).reshape(-1, d).astype(F32)
-    )
-
-    low = [a.astype(BF) for a in (dq, dk, dv)]
-    frame_query, frame_keys, frame_values = to_frames(*low)
-    d_qkv = jnp.concatenate(
-        [
-            rotate(frame_query.astype(F32), tables, -1.0).astype(BF),
-            rotate(frame_keys.astype(F32), tables, -1.0).astype(BF),
-            frame_values,
-        ],
-        axis=1,
-    )
-    d_normed_one = dot_nt(d_qkv, w_qkv)
-    entry_part, g_gain_one = rms_back(entry, inverse_one, gain_one, d_normed_one)
-    d_entry = (d_middle + entry_part).astype(BF)
-    d_entry_home = home(d_entry)
-    d_joined = dot_nt(d_entry_home, w_skip)
-    d_inputs = d_joined[:, :d].astype(BF)
-    d_skip = d_joined[:, d:].astype(BF)
-
-    head_d_qkv = jnp.concatenate(
-        [
-            rotate(low[0].astype(F32), group_tables, -1.0).astype(BF),
-            rotate(low[1].astype(F32), group_tables, -1.0).astype(BF),
-            low[2],
-        ],
-        axis=1,
-    )
-    g_qkv = dot_tn(plane_first, head_d_qkv)
-    g_skip = dot_tn(joined_own, lax.all_gather(d_entry, PLANE, axis=0, tiled=True))
-    out_qkv = finish_columns(reduce_z(g_qkv.astype(BF)))
-    out_qkv = (
-        out_qkv.reshape(parts, -1, 3, width).transpose(1, 2, 0, 3).reshape(-1, 3 * d).astype(F32)
-    )
-    out_skip = lax.all_gather(
-        reduce_z(g_skip.astype(BF)), "u", axis=0, tiled=True
-    ).astype(F32)
-
-    early = sum_all(
-        jnp.concatenate(
-            [
-                g_gain_two,
-                jnp.sum(d_up.astype(F32), axis=0),
-                jnp.sum(cotangent.astype(F32), axis=0),
-            ]
-        )
-    )
-    total_gain_one = sum_all(g_gain_one)
+        b_up.reshape(n_z, n_x, n_u, -1), (0, x, u, 0), (n_z, 1, 1, hidden // 32)
+    ).reshape(1, -1)
+    own = call_first(lens, inputs, skip_in, cotangent, w_skip, w_qkv, gain_one[None])
+    result, d_inputs, d_skip, g_skip, g_qkv, g_out, g_up, g_down, vectors = call_second(
+        own,
+        (w_out, w_up, w_down, w_qkv, w_skip),
+        (
+            gain_one[None],
+            gain_two[None],
+            b_up.reshape(8, -1),
+            b_up_own,
+            b_down[None],
+        ),
+    )
+    vectors = vectors.reshape(-1)
     return (
         result,
         d_inputs,
         d_skip,
-        out_skip,
-        total_gain_one,
-        out_qkv,
-        out_out,
-        early[:d],
-        out_up,
-        early[d : d + hidden],
-        out_down,
-        early[d + hidden :],
+        g_skip.astype(F32),
+        vectors[:d],
+        g_qkv.astype(F32),
+        g_out.astype(F32),
+        vectors[d : 2 * d],
+        g_up.astype(F32),
+        vectors[4 * d :],
+        g_down.astype(F32),
+        vectors[2 * d : 3 * d],
     )
 
 

time: 479 us -> 292 us (0.61); the launches traced: 469 us -> 291 us
  Pallas kernels: 91.9 us -> 272 us
  local copies, waits for them, and re-layouts: 110 us -> 9.5 us
  starting transfers between devices: 62.6 us -> 0 us
  matrix products: 58.4 us -> 0 us
  waiting for transfers between devices: 55.2 us -> 0 us
  other arithmetic: 47 us -> 8.96 us
  blocking collectives: 29.1 us -> 0 us
  between operations: 14.9 us -> 0.7 us
    pallas_call x1, Pallas kernels: 15.6 us -> 195 us  [call_second(): pl.pallas_call(second_kernel, in_specs=[any_space] * (len(own) + len(weig...]
    dot_general x14 -> x0, matrix products: 58.4 us -> none  [the longest x5 20.8 us: dot_tn(): lax.dot_general(a, b, (((0,), (0,)), ((), ())), preferred_element_type=F32)]
    unnamed x117 -> x21, local copies, waits for them, and re-layouts: 54.5 us -> 6.23 us
    ppermute x43 -> x0, waiting for transfers between devices: 45.2 us -> none  [the longest x33 40.1 us: permute(): return lax.ppermute(v, AXES, pairs)]
    ppermute x43 -> x0, starting transfers between devices: 45.1 us -> none  [the longest x33 28.8 us: permute(): return lax.ppermute(v, AXES, pairs)]
    all_gather x3 -> x0, blocking collectives: 29.1 us -> none  [the longest x2 21.1 us: finish_columns(): every = lax.all_gather(both, 'u', axis=0)]
    concatenate x14 -> x0, other arithmetic: 19.9 us -> none  [the longest x12 17.5 us: gather_plane(): piece = jnp.concatenate([piece, swap_plane(piece, bit)], axis=0)]
    all_to_all x3 -> x0, starting transfers between devices: 16.9 us -> none  [the longest x1 6.05 us: to_heads(): lax.all_to_all(v.reshape(frames, parts * n * width), PLANE, split_axis=1,...]
  transfers between devices with their start and end apart: 49 -> 0, of which waited for: 15 -> 0; matrix products, arithmetic and copies ran while one was open for 40% -> 0% of each run, Pallas kernels for 3% -> 0%
where the time goes in v1:
time: 292 us; the launch traced here: 291 us
  Pallas kernels  272 us (93%)
  local copies, waits for them, and re-layouts  9.5 us (3%)
  other arithmetic  8.96 us (3%)
    pallas_call x1, Pallas kernels, call_second(): pl.pallas_call(second_kernel, in_specs=[any_space] * (len(own) + len(weig...  195 us
    pallas_call x1, Pallas kernels, call_first(): pl.pallas_call(first_kernel, in_specs=[vmem] + [any_space] * 5 + [vmem],...  76.3 us
    unnamed x21, local copies, waits for them, and re-layouts  6.23 us

profile of v1, /device:TPU:5, one launch (start us, length us, event | category | flops | bytes accessed | tf_op | source)
XLA Modules:
  0.0 291.0 jit_solution(16312338120947975667)
XLA Ops:
  0.6 0.7 convert_bitcast_fusion
  1.3 1.3 dynamic-slice_bitcast_fusion.b_up_own_ref
  2.6 0.7 broadcast_in_dim.16.lens_ref
  3.3 1.3 reshape.40.b_up_ref
  4.6 76.3 %entry_to_mixed.1 = (bf16[176,1024]{1,0:T(8,128)(2,1)}, bf16[176,1024]{1,0:T(8,128)(2,1)}, bf16[1408,256]{1,0:T(8,128)(2,1)}, bf16[1408,1024]{1,0:T(8,128)(2,1)}...) custom-call(f32[8,128]{1,0:T(8,128)} %broadcast_in_dim.16.lens_ref, ...), custom_call_target="tpu_custom_call" | custom-call | tf_op jit(solution)/shard_map/entry_to_mixed/pallas_call | solution.py:573
  80.9 195.5 %mixed_to_gradients.1 = (bf16[176,1024]{1,0:T(8,128)(2,1)}, bf16[176,1024]{1,0:T(8,128)(2,1)}, bf16[176,1024]{1,0:T(8,128)(2,1)}, bf16[256,1024]{1,0:T(8,128)(2,...) custom-call(bf16[176,1024]{1,0:T(8,128)(2,1)} %get-tuple-element.34., ...), custom_call_target="tpu_custom_call" | custom-call | tf_op jit(solution)/shard_map/mixed_to_gradients/pallas_call | solution.py:1245
  276.4 0.0 copy-start.2
  276.4 0.0 copy-start.1
  276.5 0.9 slice_bitcast_fusion.1
  277.3 0.7 slice_bitcast_fusion
  278.1 0.6 copy.27
  278.7 0.6 copy.28
  279.3 0.6 copy.26
  279.9 0.6 copy.25
  280.5 1.8 convert_element_type.27
  282.2 2.1 convert_element_type.25
  284.4 0.0 copy-done.2
  284.4 0.0 copy-start
  284.4 1.3 convert_element_type.26
  285.7 0.0 copy-done.1
  285.7 0.0 copy-start.5
  285.7 0.0 copy-start.4
  285.7 1.5 convert_element_type.28
  287.2 0.0 copy-done
  287.2 0.0 copy-start.3
  287.2 1.6 convert_element_type.29
  288.8 0.0 copy-done.5
  288.8 0.7 copy.32
  289.5 0.0 copy-done.4
  289.5 0.7 copy.33
  290.3 0.0 copy-done.3
  290.3 0.7 copy.34
  (1 shorter events, 0.0 us)
Async XLA Ops:
  276.4 7.9 %copy-start.2 = (bf16[128,3072]{1,0:T(8,128)(2,1)S(1)}, bf16[128,3072]{1,0:T(8,128)(2,1)}, u32[]{:S(2)}) copy-start(bf16[128,3072]{1,0:T(8,128)(2,1)} %get-tuple-element.52) | copy-start | bytes 2359300
  276.4 9.2 %copy-start.1 = (bf16[128,4096]{1,0:T(8,128)(2,1)S(1)}, bf16[128,4096]{1,0:T(8,128)(2,1)}, u32[]{:S(2)}) copy-start(bf16[128,4096]{1,0:T(8,128)(2,1)} %get-tuple-element.54) | copy-start | bytes 3145732
  284.4 2.8 copy-start
  285.7 3.1 %copy-start.5 = (bf16[176,1024]{1,0:T(8,128)(2,1)S(1)}, bf16[176,1024]{1,0:T(8,128)(2,1)}, u32[]{:S(2)}) copy-start(bf16[176,1024]{1,0:T(8,128)(2,1)} %get-tuple-element.71) | copy-start | bytes 1081348
  285.7 3.8 %copy-start.4 = (bf16[176,1024]{1,0:T(8,128)(2,1)S(1)}, bf16[176,1024]{1,0:T(8,128)(2,1)}, u32[]{:S(2)}) copy-start(bf16[176,1024]{1,0:T(8,128)(2,1)} %get-tuple-element.72) | copy-start | bytes 1081348
  287.2 3.0 %copy-start.3 = (bf16[176,1024]{1,0:T(8,128)(2,1)S(1)}, bf16[176,1024]{1,0:T(8,128)(2,1)}, u32[]{:S(2)}) copy-start(bf16[176,1024]{1,0:T(8,128)(2,1)} %get-tuple-element.73) | copy-start | bytes 1081348
